TPU v7x, 256 devices: a whole 4x4x8 slice. The times are simulated.
256 devices in a mesh: sp: 64 (over z, x, core), dp: 4 (over y).
Axes of the slice: x: 4, y: 4, z: 8, core: 2. Of those that a mesh axis runs over, the one named last changes fastest.
Arguments:
- grid_tokens: bfloat16 [4, 64, 128, 1024], P('dp', 'sp'), may hold values from -6 to 6
- cotangent: bfloat16 [4, 64, 128, 1024], P('dp', 'sp'), may hold values from -6 to 6
- obs_pairs: bfloat16 [4, 64, 96, 2048], P('dp', 'sp'), may hold values from -6 to 6
- obs_route: int32 [4, 64, 96, 1], P('dp', 'sp'), may hold values from 0 to 63; in each aligned block of 96 rows (0 to 95, 96 to 191, ..., all dimensions but the last counted through in order) at most 3 rows name the same one
- obs_patch: int32 [4, 64, 96], P('dp', 'sp'), may hold values from 0 to 3
- w_query: bfloat16 [1024, 1024], P('dp'), may hold values from -0.1875 to 0.1875
- w_cross_out: bfloat16 [1024, 1024], P('dp'), may hold values from -0.1875 to 0.1875
- w_qkv: bfloat16 [1024, 3072], P('dp'), may hold values from -0.1875 to 0.1875
- w_axial_out: bfloat16 [1024, 1024], P('dp'), may hold values from -0.1875 to 0.1875
- w_in: bfloat16 [1024, 2048], replicated, may hold values from -0.1875 to 0.1875
- w_out: bfloat16 [2048, 1024], replicated, may hold values from -0.125 to 0.125
Outputs:
- grad_w_in: float32 [1024, 2048], P(('sp', 'dp'))
- grad_w_out: float32 [2048, 1024], P(('sp', 'dp'))
Inputs may be any that keep to these rules, and one draw needn't show every extreme that they name: `obs_route`: at most 3 of the 96 observations of one device fall in one latitude row, and in every draw some device sends exactly 3 to some row.
All inputs are finite; a program needn't handle non-finite values.
Results may differ from a plain program's by a relative error of at most 0.024.
Values may be sent and summed in bfloat16 or wider, within the bound.
A program may use at most 128 MiB of HBM per device.

v0:
```python
import jax
import jax.numpy as jnp
from jax import lax
from jax.sharding import PartitionSpec as P

HEADS = 16
PATCH = 32


norm_epsilon = 1e-06
root_half = 0.7071067811865476
inv_root_two_pi = 0.3989422804014327


def normalize(values):
    values = values.astype(jnp.float32)
    return values * lax.rsqrt(jnp.mean(values * values, axis=-1, keepdims=True) + norm_epsilon)


def gelu_exact(pre_act):
    return 0.5 * pre_act * (1.0 + jax.scipy.special.erf(pre_act * root_half))


def gelu_slope(pre_act):
    return (
        0.5 * (1.0 + jax.scipy.special.erf(pre_act * root_half))
        + pre_act * jnp.exp(-0.5 * pre_act * pre_act) * inv_root_two_pi
    )


def softmax_rows(scores):
    row_max = jnp.max(scores, axis=-1, keepdims=True)
    exp_terms = jnp.exp(scores - row_max)
    return exp_terms / jnp.sum(exp_terms, axis=-1, keepdims=True)


def local(
    grid_tokens,
    cotangent,
    obs_pairs,
    obs_route,
    obs_patch,
    w_query,
    w_cross_out,
    w_qkv,
    w_axial_out,
    w_in,
    w_out,
):
    sp_count = lax.axis_size("sp")
    lon_cells = grid_tokens.shape[2]
    model_width = grid_tokens.shape[3]
    obs_count = obs_pairs.shape[2]
    capacity = max(2, 2 * obs_count // sp_count)
    head_size = model_width // HEADS
    half_width = model_width // 2
    score_scale = head_size ** (-0.5)
    tokens = grid_tokens.reshape(lon_cells, model_width)
    full_query, full_cross_out, full_qkv, full_axial_out = (
        lax.all_gather(w_query, "dp", axis=0, tiled=True),
        lax.all_gather(w_cross_out, "dp", axis=0, tiled=True),
        lax.all_gather(w_qkv, "dp", axis=0, tiled=True),
        lax.all_gather(w_axial_out, "dp", axis=0, tiled=True),
    )
    destination = obs_route.reshape(obs_count)
    onehot = (destination[:, None] == jnp.arange(sp_count, dtype=jnp.int32)[None, :]).astype(
        jnp.int32
    )
    position_in = jnp.sum(jnp.cumsum(onehot, axis=0) * onehot, axis=1) - 1
    slot_index = destination * capacity + position_in
    send_pairs = (
        jnp.zeros((sp_count * capacity, 2 * model_width), jnp.bfloat16)
        .at[slot_index]
        .set(obs_pairs.reshape(obs_count, 2 * model_width))
    )
    send_pairs = send_pairs.reshape(sp_count, capacity, 2 * model_width)
    send_patch = (
        jnp.full((sp_count * capacity,), -1.0, jnp.float32)
        .at[slot_index]
        .set(obs_patch.reshape(obs_count).astype(jnp.float32))
    )
    send_patch = send_patch.astype(jnp.bfloat16).reshape(sp_count, capacity)
    received, received_patch = (
        lax.all_to_all(send_pairs, "sp", split_axis=0, concat_axis=0, tiled=True),
        lax.all_to_all(send_patch, "sp", split_axis=0, concat_axis=0, tiled=True),
    )
    received = received.reshape(sp_count * capacity, 2 * model_width)
    received_patch = received_patch.reshape(sp_count * capacity).astype(jnp.float32)
    normed = normalize(tokens).astype(jnp.bfloat16)
    queries = jnp.dot(normed, full_query, preferred_element_type=jnp.float32).astype(jnp.bfloat16)
    query_heads = queries.reshape(lon_cells, HEADS, head_size)
    key_heads = received[:, :model_width].reshape(-1, HEADS, head_size)
    value_heads = received[:, model_width:].reshape(-1, HEADS, head_size)
    scores = (
        jnp.einsum("lhe,she->hls", query_heads, key_heads, preferred_element_type=jnp.float32)
        * score_scale
    )
    cell_patch = (jnp.arange(lon_cells, dtype=jnp.int32) // PATCH).astype(jnp.float32)
    same_patch = received_patch[None, None, :] == cell_patch[None, :, None]
    masked = jnp.where(same_patch, scores, -1e30)
    row_max = jnp.maximum(jnp.max(masked, axis=-1, keepdims=True), 0.0)
    exp_terms = jnp.where(same_patch, jnp.exp(masked - row_max), 0.0)
    denominator = jnp.exp(-row_max) + jnp.sum(exp_terms, axis=-1, keepdims=True)
    weights = (exp_terms / denominator).astype(jnp.bfloat16)
    context = jnp.einsum("hls,she->lhe", weights, value_heads, preferred_element_type=jnp.float32)
    context = context.reshape(lon_cells, model_width).astype(jnp.bfloat16)
    after_cross = (
        tokens.astype(jnp.float32)
        + jnp.dot(context, full_cross_out, preferred_element_type=jnp.float32)
    ).astype(jnp.bfloat16)
    normed_axial = normalize(after_cross).astype(jnp.bfloat16)
    axial = jnp.dot(normed_axial, full_qkv, preferred_element_type=jnp.float32).astype(jnp.bfloat16)
    lat_part = axial[:, : 3 * half_width].reshape(1, lon_cells, HEADS // 4, 6 * head_size)
    exchanged = lax.all_to_all(lat_part, "sp", split_axis=1, concat_axis=0, tiled=True)
    lat_rows = exchanged.shape[0]
    lon_cols = exchanged.shape[1]
    group_count = exchanged.shape[2]
    split_parts = exchanged.reshape(lat_rows, lon_cols, group_count, 3, 2, head_size)
    lat_scores = (
        jnp.einsum(
            "alghe,blghe->lghab",
            split_parts[:, :, :, 0],
            split_parts[:, :, :, 1],
            preferred_element_type=jnp.float32,
        )
        * score_scale
    )
    lat_weights = softmax_rows(lat_scores).astype(jnp.bfloat16)
    lat_context = jnp.einsum(
        "lghab,blghe->alghe",
        lat_weights,
        split_parts[:, :, :, 2],
        preferred_element_type=jnp.float32,
    )
    lat_context = lat_context.astype(jnp.bfloat16).reshape(
        lat_rows, lon_cols, group_count, 2 * head_size
    )
    lat_context = lax.all_to_all(lat_context, "sp", split_axis=0, concat_axis=1, tiled=True)
    lat_context = lat_context.reshape(lon_cells, half_width)
    lon_part = axial[:, 3 * half_width :].reshape(lon_cells, 3, HEADS // 2, head_size)
    lon_scores = (
        jnp.einsum(
            "lhe,mhe->hlm", lon_part[:, 0], lon_part[:, 1], preferred_element_type=jnp.float32
        )
        * score_scale
    )
    lon_weights = softmax_rows(lon_scores).astype(jnp.bfloat16)
    lon_context = jnp.einsum(
        "hlm,mhe->lhe", lon_weights, lon_part[:, 2], preferred_element_type=jnp.float32
    )
    lon_context = lon_context.reshape(lon_cells, half_width).astype(jnp.bfloat16)
    axial_context = jnp.concatenate([lat_context, lon_context], axis=-1)
    after_axial = (
        after_cross.astype(jnp.float32)
        + jnp.dot(axial_context, full_axial_out, preferred_element_type=jnp.float32)
    ).astype(jnp.bfloat16)
    normed_ff = normalize(after_axial).astype(jnp.bfloat16)
    pre_act = jnp.dot(normed_ff, w_in, preferred_element_type=jnp.float32)
    hidden = gelu_exact(pre_act).astype(jnp.bfloat16)
    cot_rows = cotangent.reshape(lon_cells, model_width)
    grad_out_term = lax.dot_general(
        hidden, cot_rows, (((0,), (0,)), ((), ())), preferred_element_type=jnp.float32
    )
    hidden_grad = lax.dot_general(
        cot_rows, w_out, (((1,), (1,)), ((), ())), preferred_element_type=jnp.float32
    )
    pre_grad = (hidden_grad * gelu_slope(pre_act)).astype(jnp.bfloat16)
    grad_in_term = lax.dot_general(
        normed_ff, pre_grad, (((0,), (0,)), ((), ())), preferred_element_type=jnp.float32
    )
    grad_in_share, grad_out_share = (
        lax.psum_scatter(grad_in_term, ("sp", "dp"), scatter_dimension=0, tiled=True),
        lax.psum_scatter(grad_out_term, ("sp", "dp"), scatter_dimension=0, tiled=True),
    )
    return (grad_in_share, grad_out_share)


def solution(mesh):
    return jax.shard_map(
        local,
        mesh=mesh,
        in_specs=(
            P("dp", "sp", None, None),
            P("dp", "sp", None, None),
            P("dp", "sp", None, None),
            P("dp", "sp", None, None),
            P("dp", "sp", None),
            P("dp", None),
            P("dp", None),
            P("dp", None),
            P("dp", None),
            P(),
            P(),
        ),
        out_specs=(P(("sp", "dp"), None), P(("sp", "dp"), None)),
        check_vma=False,
    )
```

profile of v0, /device:TPU:2, one launch (start us, length us, event | category | flops | bytes accessed | tf_op | source)
XLA Modules:
  0.0 1758.4 jit_solution(15352307615933801830)
XLA Ops:
  7.2 0.7 all-gather.5.cloned.1.call-update
  8.0 0.7 all-gather.7.cloned.1.call-update
  8.7 0.7 all-gather.9.cloned.1.call-update
  9.7 0.2 select_reduce_fusion
  9.9 0.9 scatter_custom_fusion.1
  10.8 0.8 all_to_all.28
  11.5 12.0 all-to-all-start.1
  23.6 1.4 scatter_custom_fusion
  25.0 1.3 reshape.194
  26.4 5.7 all-to-all-done.1
  32.1 5.6 all-to-all-start
  37.7 0.5 all-gather.11.cloned.1.call-update
  38.7 27.8 %all-to-all-done = bf16[64,3,2048]{2,1,0:T(4,128)(2,1)S(1)} async-done(((bf16[64,3,2048]{2,1,0:T(4,128)(2,1)}), bf16[64,3,2048]{2,1,0:T(4,128)(2,1)S(1)}, u32[]{:S(2)}, u32[]{:S(2)}) %all-to-all-start) | async-done | bytes 786464 | tf_op jit(solution)/shard_map/all_to_all | solution.py:84
  66.5 0.7 reshape.195
  67.3 0.2 copy.35
  67.5 0.2 copy.32
  67.7 2.1 convolution_convert_fusion.3
  69.9 0.2 copy.34
  70.0 0.5 fusion.61
  70.5 0.3 fusion.5
  70.8 0.5 convolution_convert_fusion.2
  71.4 10.2 all-gather.7.cloned.1.call-done
  81.5 2.1 multiply_reduce_fusion.1
  83.7 68.0 %all-gather.9.cloned.1.call-done = bf16[1024,3072]{1,0:T(8,128)(2,1)} async-done(((bf16[256,3072]{1,0:T(8,128)(2,1)}), bf16[1024,3072]{1,0:T(8,128)(2,1)}) %all-gather.9.cloned.1.call-update) | async-done | bytes 6291472 | tf_op jit(solution)/shard_map/all_gather | solution.py:62
  151.7 3.8 convolution_convert_fusion
  155.6 0.8 reshape.199
  156.4 10.5 all-to-all-start.2
  166.9 0.2 copy.43
  167.2 0.3 convolution_multiply_fusion.1
  167.5 14.2 all-to-all-done.2
  181.8 0.4 reshape.200
  182.2 0.7 fusion.58
  182.8 0.2 copy.48
  183.0 0.3 fusion.63
  183.4 0.3 convolution_multiply_fusion.2
  183.6 0.3 convolution_convert_fusion.1
  183.9 0.8 copy.42
  184.7 6.1 all-to-all-start.3
  190.8 0.4 fusion.62
  191.2 0.3 convolution_convert_fusion.4
  191.6 9.1 all-to-all-done.3
  200.8 2.1 multiply_reduce_fusion
  202.9 3.0 fusion.57
  205.9 8.1 fusion.6
  214.1 4.5 fusion.22
  218.6 269.6 %all-reduce.3.cloned.1.call-done = f32[1024,2048]{1,0:T(8,128)} async-done(((f32[1024,2048]{1,0:T(8,128)}), f32[1024,2048]{1,0:T(8,128)}) %all-reduce.3.cloned.1.call-update) | async-done | bytes 8388624
  488.3 1.5 constant_dynamic-slice_fusion
  489.7 1261.8 %reduce-scatter.2.cloned.1.call-done = f32[8,1024]{1,0:T(8,128)} async-done(((f32[2048,1024]{1,0:T(8,128)}), f32[8,1024]{1,0:T(8,128)}) %reduce-scatter.2.cloned.1.call-update) | async-done | bytes 32784 | tf_op jit(solution)/shard_map/reduce_scatter | solution.py:173
  (42 shorter events, 1.4 us)
Async XLA Ops:
  7.2 16.4 copy-start
  7.2 2.2 copy-start.4
  7.2 2.6 copy-start.5
  7.2 60.5 %all-gather.5.cloned.1.call-start = ((), (), s32[]{:S(2)}) async-start(), calls=%async_computation.5 | async-start | bytes 2621440 | tf_op jit(solution)/shard_map/all_gather | solution.py:60
  7.9 73.6 %all-gather.7.cloned.1.call-start = ((), (), s32[]{:S(2)}) async-start(), calls=%async_computation.6 | async-start | bytes 2621440 | tf_op jit(solution)/shard_map/all_gather | solution.py:61
  8.7 143.0 %all-gather.9.cloned.1.call-start = ((), (), s32[]{:S(2)}) async-start(), calls=%async_computation.7 | async-start | bytes 7864320 | tf_op jit(solution)/shard_map/all_gather | solution.py:62
  11.5 20.5 %all-to-all-start.1 = ((bf16[64,1,3]{2,1,0:T(2,128)(2,1)}), bf16[64,1,3]{2,1,0:T(2,128)(2,1)S(1)}, u32[]{:S(2)}, u32[]{:S(2)}) async-start(bf16[64,1,3]{2,1,0:T(2,128)(2,1)} %all_to_all.28), calls=%async_computation.1 | async-start | bytes 65536 | tf_op jit(solution)/shard_map/all_to_all | solution.py:85
  25.0 13.2 copy-start.2
  32.1 34.5 %all-to-all-start = ((bf16[64,3,2048]{2,1,0:T(4,128)(2,1)}), bf16[64,3,2048]{2,1,0:T(4,128)(2,1)S(1)}, u32[]{:S(2)}, u32[]{:S(2)}) async-start(bf16[64,3,2048]{2,1,0:T(4,128)(2,1)} %reshape.194), calls=%async_computation | async-start | bytes 2097152 | tf_op jit(solution)/shard_map/all_to_all | solution.py:84
  37.6 163.1 %all-gather.11.cloned.1.call-start = ((), (), s32[]{:S(2)}) async-start(), calls=%async_computation.8 | async-start | bytes 2621440 | tf_op jit(solution)/shard_map/all_gather | solution.py:63
  156.4 25.3 %all-to-all-start.2 = ((bf16[1,128,4,384]{3,2,0,1:T(4,128)(2,1)}), bf16[1,128,4,384]{3,2,0,1:T(4,128)(2,1)S(1)}, u32[]{:S(2)}, u32[]{:S(2)}) async-start(bf16[1,128,4,384]{3,2,0,1:T(4,128)(2,1)} %bitcast.13), calls=%async_computation.2 | async-start | bytes 786432 | tf_op jit(solution)/shard_map/all_to_all | solution.py:114
  184.7 16.0 all-to-all-start.3
  190.8 297.5 %all-reduce.3.cloned.1.call-start = ((), (), s32[]{:S(2)}) async-start(), calls=%async_computation.10 | async-start | bytes 16777216
  202.9 3.0 copy-start.3
  214.0 1537.5 %reduce-scatter.2.cloned.1.call-start = ((), (), s32[]{:S(2)}) async-start(), calls=%async_computation.9 | async-start | bytes 8421376 | tf_op jit(solution)/shard_map/reduce_scatter | solution.py:173
  218.6 1532.9 %copy-start.1 = (bf16[1,1,96,2048]{3,2,1,0:T(8,128)(2,1)S(1)}, bf16[1,1,96,2048]{3,2,1,0:T(8,128)(2,1)}, u32[]{:S(2)}) copy-start(bf16[1,1,96,2048]{3,2,1,0:T(8,128)(2,1)} %param.13) | copy-start | bytes 1179652
Sparse Core Ops, SparseCore 0:
  9.8 36.3 all-gather.4
  48.1 33.4 all-gather.6
  83.3 68.2 all-gather.8
  153.4 34.0 all-gather.10
  214.1 274.0 all-reduce.2
  491.3 1260.1 reduce-scatter.1
where the time goes:
time: 1780 us; the launch traced here: 1760 us
  waiting for transfers between devices  1670 us (94%)
  starting transfers between devices  34.5 us (2%)
  matrix products  28.5 us (2%)
    reduce_scatter x1, waiting for transfers between devices, local(): lax.psum_scatter(grad_out_term, ('sp', 'dp'), scatter_dimension=0, tiled=...  1260 us
    unnamed x7, waiting for transfers between devices  272 us
    all_gather x1, waiting for transfers between devices, local(): lax.all_gather(w_qkv, 'dp', axis=0, tiled=True)  68 us
  transfers between devices with their start and end apart: 10, of which 8 were waited for; matrix products, arithmetic and copies ran while one was open for 1% of the time, Pallas kernels for 0%

commit v1 on v0

v1 whole, which is shorter than its diff:
```python
import jax
import jax.numpy as jnp
from jax import lax
from jax.experimental import pallas as pl
from jax.experimental.pallas import tpu as pltpu
from jax.sharding import PartitionSpec as P

BF = jnp.bfloat16
F32 = jnp.float32
EPS = 1e-06
ROOT_HALF = 0.7071067811865476
INV_ROOT_TWO_PI = 0.3989422804014327
SCALE = 0.125


def normalize(values):
    values = values.astype(F32)
    return values * lax.rsqrt(jnp.mean(values * values, axis=-1, keepdims=True) + EPS)


def dot(a, b):
    return jnp.dot(a, b, preferred_element_type=F32)


def dot_t(a, b):
    return lax.dot_general(a, b, (((1,), (1,)), ((), ())), preferred_element_type=F32)


def mult(value, by):
    return pl.multiple_of(value, by)


def push(src, dst, send, recv, sp, dp):
    pltpu.make_async_remote_copy(
        src_ref=src,
        dst_ref=dst,
        send_sem=send,
        recv_sem=recv,
        device_id={"sp": sp, "dp": dp},
        device_id_type=pl.DeviceIdType.MESH,
    ).start()


def await_bytes(ref, sem):
    pltpu.make_async_copy(ref, ref, sem).wait()


def kernel(
    src_index,
    tokens,
    cot,
    pairs,
    slot_patch,
    wq_hbm,
    wc_hbm,
    wkv_hbm,
    wa_hbm,
    wi_hbm,
    wo_hbm,
    out_in,
    out_out,
    wq,
    wc,
    wkv,
    wa,
    wi,
    wo,
    obs_send,
    obs_recv,
    obs_wide,
    patch_recv,
    queries,
    context,
    after_cross,
    axial,
    lat_own,
    lat_sib,
    q_wide,
    k_wide,
    v_wide,
    ks_wide,
    vs_wide,
    o_wide,
    lat_out,
    lat_context,
    lon_context,
    normed_all,
    cot_all,
    hidden_t,
    pre_grad_t,
    gin_send,
    gout_send,
    gin_recv,
    gout_recv,
    fin_in_send,
    fin_in_recv,
    fin_out_send,
    fin_out_recv,
    local_sem,
    w_send,
    w_recv,
    f_send,
    f_recv,
    gather_send,
    gather_recv,
    share_send,
    share_recv,
    bulk_send,
    bulk_recv,
    last_send,
    last_in,
    last_out,
):
    sp = lax.axis_index("sp")
    y = lax.axis_index("dp")
    core = sp % 2
    sib = sp + 1 - 2 * core
    chip = sp // 2
    x = chip % 4
    z = chip // 4
    part = sp % 8

    pieces = (
        (wq_hbm, wq, 0, 1024),
        (wc_hbm, wc, 0, 1024),
        (wkv_hbm, wkv, 0, 1536),
        (wkv_hbm, wkv, 1536, 1536),
        (wa_hbm, wa, 0, 1024),
    )

    def start_piece(i):
        hbm, full, col, width = pieces[i]
        for k in range(1, 4):
            push(
                hbm.at[pl.ds(mult(core * 128, 128), 128), pl.ds(col, width)],
                full.at[pl.ds(mult(y * 256 + core * 128, 128), 128), pl.ds(col, width)],
                w_send.at[i],
                w_recv.at[i, k - 1],
                sp,
                (y + k) % 4,
            )

    def own_piece(i):
        hbm, full, col, width = pieces[i]
        return pltpu.make_async_copy(
            hbm.at[:, pl.ds(col, width)],
            full.at[pl.ds(mult(y * 256, 256), 256), pl.ds(col, width)],
            local_sem.at[i],
        )

    def forward_piece(i):
        hbm, full, col, width = pieces[i]
        for k in range(1, 4):
            rows = full.at[
                pl.ds(mult(((y - k + 4) % 4) * 256 + core * 128, 128), 128), pl.ds(col, width)
            ]
            await_bytes(rows, w_recv.at[i, k - 1])
            push(rows, rows, f_send.at[i], f_recv.at[i], sib, y)

    def finish_piece(i):
        hbm, full, col, width = pieces[i]
        await_bytes(full.at[pl.ds(0, 384), pl.ds(col, width)], f_recv.at[i])
        own_piece(i).wait()

    def drain_piece(i):
        hbm, full, col, width = pieces[i]
        await_bytes(full.at[pl.ds(0, 384), pl.ds(col, width)], w_send.at[i])
        await_bytes(full.at[pl.ds(0, 384), pl.ds(col, width)], f_send.at[i])

    start_piece(0)
    for i in range(5):
        own_piece(i).start()
    wi_copy = pltpu.make_async_copy(
        wi_hbm.at[:, pl.ds(mult(part * 256, 256), 256)], wi, local_sem.at[5]
    )
    wo_copy = pltpu.make_async_copy(
        wo_hbm.at[pl.ds(mult(part * 256, 256), 256), :], wo, local_sem.at[6]
    )
    wi_copy.start()
    wo_copy.start()

    def place(s, carry):
        obs_send[s] = pairs[src_index[s]]
        return carry

    lax.fori_loop(0, 192, place, 0, unroll=8)

    def send_obs(k, carry):
        to = (sp + k) % 64
        push(
            obs_send.at[pl.ds(to * 3, 3)],
            obs_recv.at[pl.ds(sp * 3, 3)],
            bulk_send.at[0],
            bulk_recv.at[0],
            to,
            y,
        )
        push(slot_patch.at[to], patch_recv.at[sp], bulk_send.at[1], bulk_recv.at[1], to, y)
        return carry

    lax.fori_loop(1, 64, send_obs, 0)
    obs_recv[pl.ds(sp * 3, 3)] = obs_send[pl.ds(sp * 3, 3)]
    patch_recv[sp] = slot_patch[sp]
    start_piece(1)

    def share_start(j, source, full):
        rows = full.at[pl.ds(mult(part * 128, 128), 128), :]
        push(source, rows, gather_send.at[j], gather_recv.at[j, 0], sib, y)
        for k in range(1, 4):
            push(
                source,
                rows,
                gather_send.at[j],
                gather_recv.at[j, k],
                z * 8 + ((x + k) % 4) * 2 + core,
                y,
            )

    def share_forward(j, full):
        for k in range(1, 4):
            rows = full.at[pl.ds(mult((((x - k + 4) % 4) * 2 + core) * 128, 128), 128), :]
            await_bytes(rows, gather_recv.at[j, k])
            push(rows, rows, share_send.at[j], share_recv.at[j], sib, y)

    def share_finish(j, full):
        await_bytes(full.at[pl.ds(0, 128), :], gather_recv.at[j, 0])
        await_bytes(full.at[pl.ds(0, 384), :], share_recv.at[j])

    def share_drain(j, full):
        await_bytes(full.at[pl.ds(0, 512), :], gather_send.at[j])
        await_bytes(full.at[pl.ds(0, 384), :], share_send.at[j])

    start_piece(2)
    share_start(0, cot, cot_all)
    cot_all[pl.ds(mult(part * 128, 128), 128), :] = cot[...]
    start_piece(3)
    start_piece(4)

    normed = normalize(tokens[...]).astype(BF)
    forward_piece(0)
    finish_piece(0)

    def columns(count, width, source, weight, target, offset):
        def step(n, carry):
            cols = pl.ds(mult(offset + n * width, width), width)
            target[:, cols] = dot(source, weight[:, cols]).astype(BF)
            return carry

        lax.fori_loop(0, count, step, 0)

    columns(4, 256, normed, wq, queries, 0)

    await_bytes(obs_recv.at[pl.ds(0, 189)], bulk_recv.at[0])
    await_bytes(patch_recv.at[pl.ds(0, 63)], bulk_recv.at[1])
    obs_wide[...] = obs_recv[...].astype(F32).reshape(3072, 128)
    patches = patch_recv[...].reshape(64, 128)
    slot_lane = lax.broadcasted_iota(jnp.int32, (64, 192), 1)
    slot_from = lax.broadcasted_iota(jnp.int32, (64, 192), 0) * 3
    slot_row = jnp.zeros((1, 192), F32)
    for r in range(3):
        slot_row += jnp.sum(
            jnp.where(slot_lane == slot_from + r, patches[:, r : r + 1], 0.0),
            axis=0,
            keepdims=True,
        )
    cell_patch = (lax.broadcasted_iota(jnp.int32, (128, 192), 0) // 32).astype(F32)
    same_patch = cell_patch == slot_row
    low = lax.broadcasted_iota(jnp.int32, (128, 128), 1) < 64
    zero = jnp.zeros((128, 128), BF)

    def cross_pair(g, carry):
        cols = pl.ds(mult(g * 128, 128), 128)
        keys = obs_wide[pl.ds(g, 192, stride=16), :].astype(BF)
        values = obs_wide[pl.ds(g + 8, 192, stride=16), :].astype(BF)
        both = queries[:, cols]
        found = []
        for half in (jnp.where(low, both, zero), jnp.where(low, zero, both)):
            masked = jnp.where(same_patch, dot_t(half, keys) * SCALE, -1e30)
            top = jnp.maximum(jnp.max(masked, axis=-1, keepdims=True), 0.0)
            terms = jnp.where(same_patch, jnp.exp(masked - top), 0.0)
            total = jnp.exp(-top) + jnp.sum(terms, axis=-1, keepdims=True)
            found.append(dot((terms / total).astype(BF), values))
        context[:, cols] = jnp.where(low, found[0], found[1]).astype(BF)
        return carry

    lax.fori_loop(0, 8, cross_pair, 0)

    forward_piece(1)
    finish_piece(1)

    def cross_out(n, carry):
        cols = pl.ds(mult(n * 256, 256), 256)
        after_cross[:, cols] = (
            tokens[:, cols].astype(F32) + dot(context[...], wc[:, cols])
        ).astype(BF)
        return carry

    lax.fori_loop(0, 4, cross_out, 0)
    normed_axial = normalize(after_cross[...]).astype(BF)
    forward_piece(2)
    finish_piece(2)
    columns(6, 256, normed_axial, wkv, axial, 0)

    cell_at, group_at = z, x

    def send_lat(k, carry):
        to = (chip + k) % 32
        push(
            axial.at[pl.ds(mult((to // 4) * 16, 16), 16), pl.ds(mult((to % 4) * 384, 128), 384)],
            lat_own.at[chip],
            bulk_send.at[2],
            bulk_recv.at[2],
            to * 2 + core,
            y,
        )
        return carry

    lax.fori_loop(1, 32, send_lat, 0)
    lat_own[chip] = axial[pl.ds(mult(cell_at * 16, 16), 16), pl.ds(mult(group_at * 384, 128), 384)]

    share_forward(0, cot_all)

    forward_piece(3)
    finish_piece(3)
    columns(6, 256, normed_axial, wkv, axial, 1536)

    def lon_pair(p, carry):
        both = axial[:, pl.ds(mult(1536 + p * 128, 128), 128)]
        keys = axial[:, pl.ds(mult(2048 + p * 128, 128), 128)]
        values = axial[:, pl.ds(mult(2560 + p * 128, 128), 128)]
        found = []
        for half in (jnp.where(low, both, zero), jnp.where(low, zero, both)):
            scores = dot_t(half, keys) * SCALE
            terms = jnp.exp(scores - jnp.max(scores, axis=-1, keepdims=True))
            weights = (terms / jnp.sum(terms, axis=-1, keepdims=True)).astype(BF)
            found.append(dot(weights, values))
        lon_context[:, pl.ds(mult(p * 128, 128), 128)] = jnp.where(low, found[0], found[1]).astype(
            BF
        )
        return carry

    lat_kv = lat_own.at[:, :, pl.ds(128, 256)]
    await_bytes(lat_own.at[pl.ds(0, 31)], bulk_recv.at[2])
    push(lat_kv, lat_sib, bulk_send.at[3], bulk_recv.at[3], sib, y)
    lax.fori_loop(0, 4, lon_pair, 0)
    q_wide[...] = lat_own[:, :, 0:128].astype(F32).reshape(512, 128)
    k_wide[...] = lat_own[:, :, 128:256].astype(F32).reshape(512, 128)
    v_wide[...] = lat_own[:, :, 256:384].astype(F32).reshape(512, 128)
    await_bytes(lat_sib, bulk_recv.at[3])
    ks_wide[...] = lat_sib[:, :, 0:128].astype(F32).reshape(512, 128)
    vs_wide[...] = lat_sib[:, :, 128:256].astype(F32).reshape(512, 128)
    low_rows = lax.broadcasted_iota(jnp.int32, (32, 128), 1) < 64

    def lat_cell(l, carry):
        rows = pl.ds(l, 32, stride=16)
        q = q_wide[rows, :]
        both = jnp.concatenate(
            [jnp.where(low_rows, q, 0.0), jnp.where(low_rows, 0.0, q)], axis=0
        ).astype(BF)
        keys = jnp.concatenate([k_wide[rows, :], ks_wide[rows, :]], axis=0).astype(BF)
        values = jnp.concatenate([v_wide[rows, :], vs_wide[rows, :]], axis=0).astype(BF)
        scores = dot_t(both, keys) * SCALE
        terms = jnp.exp(scores - jnp.max(scores, axis=-1, keepdims=True))
        weights = (terms / jnp.sum(terms, axis=-1, keepdims=True)).astype(BF)
        found = dot(weights, values)
        o_wide[rows, :] = jnp.where(low_rows, found[:32], found[32:])
        return carry

    lax.fori_loop(0, 16, lat_cell, 0, unroll=4)
    lat_out[...] = o_wide[...].reshape(32, 16, 128).astype(BF)
    home = (pl.ds(mult(cell_at * 16, 16), 16), pl.ds(mult(group_at * 128, 128), 128))

    def send_back(k, carry):
        to = (chip + k) % 32
        push(
            lat_out.at[to],
            lat_context.at[home],
            bulk_send.at[4],
            bulk_recv.at[4],
            to * 2 + core,
            y,
        )
        return carry

    lax.fori_loop(1, 32, send_back, 0)
    lat_context[home] = lat_out[chip]
    forward_piece(4)
    finish_piece(4)
    await_bytes(lat_out.at[pl.ds(0, 31)], bulk_recv.at[4])

    mine = pl.ds(mult(part * 128, 128), 128)

    def axial_out(n, carry):
        cols = pl.ds(mult(n * 256, 256), 256)
        context[:, cols] = (
            after_cross[:, cols].astype(F32)
            + dot(lat_context[...], wa[pl.ds(0, 512), cols])
            + dot(lon_context[...], wa[pl.ds(512, 512), cols])
        ).astype(BF)
        return carry

    lax.fori_loop(0, 4, axial_out, 0)
    normed_all[mine, :] = normalize(context[...]).astype(BF)
    share_start(1, normed_all.at[mine, :], normed_all)
    share_finish(0, cot_all)
    wi_copy.wait()
    wo_copy.wait()
    share_forward(1, normed_all)
    share_finish(1, normed_all)

    def ff_rows(n, carry):
        rows = pl.ds(mult(n * 256, 256), 256)
        pre_act = dot(normed_all[rows, :], wi[...])
        hidden_grad = dot_t(cot_all[rows, :], wo[...])
        cdf = 0.5 * (1.0 + lax.erf(pre_act * ROOT_HALF))
        slope = cdf + pre_act * jnp.exp(-0.5 * pre_act * pre_act) * INV_ROOT_TWO_PI
        hidden_t[:, rows] = (pre_act * cdf).astype(BF).T
        pre_grad_t[:, rows] = (hidden_grad * slope).astype(BF).T
        return carry

    lax.fori_loop(0, 4, ff_rows, 0)

    def grad_cols(n, carry):
        cols = pl.ds(mult(n * 256, 256), 256)
        gout_send[:, cols] = dot(hidden_t[...], cot_all[:, cols]).astype(BF)
        gin_send[cols, :] = dot(pre_grad_t[...], normed_all[:, cols]).astype(BF).T
        return carry

    lax.fori_loop(0, 4, grad_cols, 0)

    place_at = z * 4 + y

    def blocks(to):
        return (
            (pl.ds(mult(to * 32, 32), 32), slice(None)),
            (pl.ds(mult((to // 2) * 16, 16), 16), pl.ds(mult((to % 2) * 512, 512), 512)),
        )

    def send_grads(k, carry):
        to = (place_at + k) % 32
        at_in, at_out = blocks(to)
        to_sp, to_dp = (to // 4) * 8 + part, to % 4
        push(
            gin_send.at[at_in],
            gin_recv.at[place_at],
            bulk_send.at[5],
            bulk_recv.at[5],
            to_sp,
            to_dp,
        )
        push(
            gout_send.at[at_out],
            gout_recv.at[place_at],
            bulk_send.at[6],
            bulk_recv.at[6],
            to_sp,
            to_dp,
        )
        return carry

    lax.fori_loop(1, 32, send_grads, 0)
    at_in, at_out = blocks(place_at)
    gin_recv[place_at] = gin_send[at_in]
    gout_recv[place_at] = gout_send[at_out]
    await_bytes(gin_recv.at[pl.ds(0, 31)], bulk_recv.at[5])
    await_bytes(gout_recv.at[pl.ds(0, 31)], bulk_recv.at[6])

    def add_in(n, total):
        return total + gin_recv[n].astype(F32)

    def add_out(n, total):
        return total + gout_recv[n].astype(F32)

    sum_in = lax.fori_loop(0, 32, add_in, jnp.zeros((32, 256), F32), unroll=4)
    sum_out = lax.fori_loop(0, 32, add_out, jnp.zeros((16, 512), F32), unroll=4)
    for n in range(8):
        fin_in_send[n] = sum_in[n * 4 : n * 4 + 4]
    for n in range(2):
        fin_out_send[n] = sum_out[n * 8 : n * 8 + 8]

    for n in range(8):
        to_sp, to_dp = z * 8 + y * 2 + n // 4, n % 4
        here = (to_sp == sp) & (to_dp == y)

        @pl.when(here)
        def _():
            fin_in_recv[part] = fin_in_send[n]

        @pl.when(jnp.logical_not(here))
        def _():
            push(
                fin_in_send.at[n],
                fin_in_recv.at[part],
                last_send.at[n],
                last_in.at[part],
                to_sp,
                to_dp,
            )

    for n in range(2):
        to_sp, to_dp = part * 8 + z, (y // 2) * 2 + n
        here = (to_sp == sp) & (to_dp == y)

        @pl.when(here)
        def _():
            fin_out_recv[y % 2] = fin_out_send[n]

        @pl.when(jnp.logical_not(here))
        def _():
            push(
                fin_out_send.at[n],
                fin_out_recv.at[y % 2],
                last_send.at[8 + n],
                last_out.at[y % 2],
                to_sp,
                to_dp,
            )

    for n in range(8):
        from_sp, from_dp = z * 8 + n, part // 2

        @pl.when(jnp.logical_not((from_sp == sp) & (from_dp == y)))
        def _():
            await_bytes(fin_in_recv.at[n], last_in.at[n])

        out_in[:, n * 256 : (n + 1) * 256] = fin_in_recv[n]
    for n in range(2):
        from_sp, from_dp = part * 8 + z, (y // 2) * 2 + n

        @pl.when(jnp.logical_not((from_sp == sp) & (from_dp == y)))
        def _():
            await_bytes(fin_out_recv.at[n], last_out.at[n])

        out_out[:, n * 512 : (n + 1) * 512] = fin_out_recv[n]

    for i in range(5):
        drain_piece(i)
    share_drain(0, cot_all)
    share_drain(1, normed_all)
    await_bytes(obs_recv.at[pl.ds(0, 189)], bulk_send.at[0])
    await_bytes(patch_recv.at[pl.ds(0, 63)], bulk_send.at[1])
    await_bytes(lat_own.at[pl.ds(0, 31)], bulk_send.at[2])
    await_bytes(lat_sib, bulk_send.at[3])
    await_bytes(lat_out.at[pl.ds(0, 31)], bulk_send.at[4])
    await_bytes(gin_recv.at[pl.ds(0, 31)], bulk_send.at[5])
    await_bytes(gout_recv.at[pl.ds(0, 31)], bulk_send.at[6])
    for n in range(8):
        to_sp, to_dp = z * 8 + y * 2 + n // 4, n % 4

        @pl.when(jnp.logical_not((to_sp == sp) & (to_dp == y)))
        def _():
            await_bytes(fin_in_send.at[n], last_send.at[n])

    for n in range(2):
        to_sp, to_dp = part * 8 + z, (y // 2) * 2 + n

        @pl.when(jnp.logical_not((to_sp == sp) & (to_dp == y)))
        def _():
            await_bytes(fin_out_send.at[n], last_send.at[8 + n])


def scratch():
    vmem = pltpu.VMEM
    dma = pltpu.SemaphoreType.DMA
    return [
        vmem((1024, 1024), BF),
        vmem((1024, 1024), BF),
        vmem((1024, 3072), BF),
        vmem((1024, 1024), BF),
        vmem((1024, 256), BF),
        vmem((256, 1024), BF),
        vmem((192, 16, 128), BF),
        vmem((192, 16, 128), BF),
        vmem((3072, 128), F32),
        vmem((64, 1, 128), F32),
        vmem((128, 1024), BF),
        vmem((128, 1024), BF),
        vmem((128, 1024), BF),
        vmem((128, 3072), BF),
        vmem((32, 16, 384), BF),
        vmem((32, 16, 256), BF),
        vmem((512, 128), F32),
        vmem((512, 128), F32),
        vmem((512, 128), F32),
        vmem((512, 128), F32),
        vmem((512, 128), F32),
        vmem((512, 128), F32),
        vmem((32, 16, 128), BF),
        vmem((128, 512), BF),
        vmem((128, 512), BF),
        vmem((1024, 1024), BF),
        vmem((1024, 1024), BF),
        vmem((256, 1024), BF),
        vmem((256, 1024), BF),
        vmem((1024, 256), BF),
        vmem((256, 1024), BF),
        vmem((32, 32, 256), BF),
        vmem((32, 16, 512), BF),
        vmem((8, 4, 256), F32),
        vmem((8, 4, 256), F32),
        vmem((2, 8, 512), F32),
        vmem((2, 8, 512), F32),
        dma((7,)),
        dma((5,)),
        dma((5, 3)),
        dma((5,)),
        dma((5,)),
        dma((2,)),
        dma((2, 4)),
        dma((2,)),
        dma((2,)),
        dma((7,)),
        dma((7,)),
        dma((10,)),
        dma((8,)),
        dma((2,)),
    ]


def local(
    grid_tokens,
    cotangent,
    obs_pairs,
    obs_route,
    obs_patch,
    w_query,
    w_cross_out,
    w_qkv,
    w_axial_out,
    w_in,
    w_out,
):
    row = obs_route.reshape(96)
    order = jnp.arange(96, dtype=jnp.int32)
    earlier = (row[:, None] == row[None, :]) & (order[None, :] < order[:, None])
    slot = row * 3 + jnp.sum(earlier.astype(jnp.int32), axis=1)
    hit = slot[None, :] == jnp.arange(192, dtype=jnp.int32)[:, None]
    src_index = jnp.sum(jnp.where(hit, order[None, :], 0), axis=1)
    patch = jnp.sum(jnp.where(hit, obs_patch.reshape(1, 96) + 1, 0), axis=1) - 1
    slot_patch = jnp.pad(patch.astype(F32).reshape(64, 1, 3), ((0, 0), (0, 0), (0, 125)))
    vmem = pl.BlockSpec(memory_space=pltpu.VMEM)
    hbm = pl.BlockSpec(memory_space=pl.ANY)
    return pl.pallas_call(
        kernel,
        out_shape=(
            jax.ShapeDtypeStruct((4, 2048), F32),
            jax.ShapeDtypeStruct((8, 1024), F32),
        ),
        in_specs=[pl.BlockSpec(memory_space=pltpu.SMEM)] + [vmem] * 4 + [hbm] * 6,
        out_specs=(vmem, vmem),
        scratch_shapes=scratch(),
        compiler_params=pltpu.CompilerParams(
            has_side_effects=True, vmem_limit_bytes=50 * 1024 * 1024
        ),
    )(
        src_index,
        grid_tokens.reshape(128, 1024),
        cotangent.reshape(128, 1024),
        obs_pairs.reshape(96, 16, 128),
        slot_patch,
        w_query,
        w_cross_out,
        w_qkv,
        w_axial_out,
        w_in,
        w_out,
    )


def solution(mesh):
    return jax.shard_map(
        local,
        mesh=mesh,
        in_specs=(
            P("dp", "sp", None, None),
            P("dp", "sp", None, None),
            P("dp", "sp", None, None),
            P("dp", "sp", None, None),
            P("dp", "sp", None),
            P("dp", None),
            P("dp", None),
            P("dp", None),
            P("dp", None),
            P(),
            P(),
        ),
        out_specs=(P(("sp", "dp"), None), P(("sp", "dp"), None)),
        check_vma=False,
    )
```

time: 1780 us -> 160 us (0.09); the launches traced: 1760 us -> 159 us
  waiting for transfers between devices: 1670 us -> 0 us
  Pallas kernels: 0 us -> 148 us
  starting transfers between devices: 34.5 us -> 0 us
  matrix products: 28.5 us -> 0 us
    reduce_scatter x1 -> x0, waiting for transfers between devices: 1260 us -> none  [local(): lax.psum_scatter(grad_out_term, ('sp', 'dp'), scatter_dimension=0, tiled=...]
    unnamed x7 -> x0, waiting for transfers between devices: 272 us -> none
    pallas_call x0 -> x1, Pallas kernels: none -> 148 us  [local(): pl.pallas_call(kernel, out_shape=(jax.ShapeDtypeStruct((4, 2048), F32), j...]
    all_gather x4 -> x0, waiting for transfers between devices: 78.2 us -> none  [the longest x1 68 us: local(): lax.all_gather(w_qkv, 'dp', axis=0, tiled=True)]
    all_to_all x4 -> x0, waiting for transfers between devices: 56.9 us -> none  [the longest x1 27.8 us: local(): lax.all_to_all(send_pairs, 'sp', split_axis=0, concat_axis=0, tiled=True)]
    all_to_all x4 -> x0, starting transfers between devices: 34.2 us -> none  [the longest x1 12 us: local(): lax.all_to_all(send_patch, 'sp', split_axis=0, concat_axis=0, tiled=True)]
    dot_general x13 -> x0, matrix products: 27.8 us -> none  [the longest x1 8.06 us: local(): lax.dot_general(normed_ff, pre_grad, (((0,), (0,)), ((), ())), preferred_...]
  transfers between devices with their start and end apart: 10 -> 0, of which waited for: 8 -> 0; matrix products, arithmetic and copies ran while one was open for 1% -> 0% of each run, Pallas kernels for 0% -> 0%
where the time goes in v1:
time: 160 us; the launch traced here: 159 us
  Pallas kernels  148 us (92%)
  local copies, waits for them, and re-layouts  7.47 us (5%)
  other arithmetic  2.4 us (2%)
    pallas_call x1, Pallas kernels, local(): pl.pallas_call(kernel, out_shape=(jax.ShapeDtypeStruct((4, 2048), F32), j...  148 us
    unnamed x13, local copies, waits for them, and re-layouts  7.31 us

profile of v1, /device:TPU:2, one launch (start us, length us, event | category | flops | bytes accessed | tf_op | source)
XLA Modules:
  0.0 158.8 jit_solution(2708222026657697012)
XLA Ops:
  0.6 0.7 add_bitcast_fusion
  1.3 0.9 convert_reduce_fusion
  2.2 0.7 multiply_add_fusion
  2.9 0.2 select_reduce_fusion
  3.0 0.1 convert_element_type.20
  3.2 1.1 copy.15
  4.3 0.0 copy-start
  4.3 1.0 copy-done
  5.3 0.0 copy-start.1
  5.3 1.0 copy-done.1
  6.4 0.0 copy-start.2
  6.4 1.0 copy-done.2
  7.4 0.0 copy-start.3
  7.4 0.9 copy-done.3
  8.4 0.0 copy-start.4
  8.4 0.9 copy-done.4
  9.3 148.3 %shard_map.122 = (f32[4,2048]{1,0:T(4,128)S(1)}, f32[8,1024]{1,0:T(8,128)S(1)}) custom-call(s32[192]{0:T(256)S(1)} %get-tuple-element.3.src_index, bf16[128,1024]{1,0:T(8,128)(2,1)S(1)} %bitcast.12, bf16[128,1024]{1,0:T(8,128)(2,1)S(1)} %bitcast.13, bf16[96,16,128]{2,1,0:T(8,128)(2,1)S(1)} %bitcast.11, f32[64,1,128]{2,1,0:T(1,128)S(1)} %pad.4.slot_patch, ...), custom_call_target="tpu_custom_call" | custom-call | tf_op jit(solution)/shard_map/pallas_call | solution.py:643
  157.6 0.6 copy.18
  158.2 0.6 copy.19
  (2 shorter events, 0.0 us)
Async XLA Ops:
  4.3 1.0 copy-start
  5.3 1.0 copy-start.1
  6.4 1.0 copy-start.2
  7.4 0.9 copy-start.3
  8.4 0.9 copy-start.4

commit v2 on v1

--- a/solution.py
+++ b/solution.py
@@ -46,11 +46,11 @@
 
 
 def kernel(
-    src_index,
-    tokens,
-    cot,
-    pairs,
-    slot_patch,
+    tokens_hbm,
+    cot_hbm,
+    pairs_hbm,
+    route_hbm,
+    patch_hbm,
     wq_hbm,
     wc_hbm,
     wkv_hbm,
@@ -59,6 +59,16 @@
     wo_hbm,
     out_in,
     out_out,
+    tokens,
+    cot,
+    pairs,
+    route,
+    patch,
+    pairs_wide,
+    pairs_tiles,
+    index_row,
+    src_index,
+    slot_patch,
     wq,
     wc,
     wkv,
@@ -99,8 +109,6 @@
     local_sem,
     w_send,
     w_recv,
-    f_send,
-    f_recv,
     gather_send,
     gather_recv,
     share_send,
@@ -120,6 +128,44 @@
     z = chip // 4
     part = sp % 8
 
+    barrier = pltpu.get_barrier_semaphore()
+
+    def greet(to_sp, to_dp):
+        pl.semaphore_signal(
+            barrier,
+            inc=1,
+            device_id={"sp": to_sp, "dp": to_dp},
+            device_id_type=pl.DeviceIdType.MESH,
+        )
+
+    def greet_row(k, carry):
+        greet((sp + k) % 64, y)
+        return carry
+
+    def greet_member(k, carry):
+        for other in range(1, 4):
+            greet(k * 8 + part, (y + other) % 4)
+        return carry
+
+    lax.fori_loop(1, 64, greet_row, 0)
+    lax.fori_loop(0, 8, greet_member, 0)
+    greet(part * 8 + z, y + 1 - 2 * (y % 2))
+
+    loads = [
+        pltpu.make_async_copy(source, target, local_sem.at[7 + i])
+        for i, (source, target) in enumerate(
+            (
+                (route_hbm, route),
+                (patch_hbm, patch),
+                (pairs_hbm, pairs),
+                (tokens_hbm, tokens),
+                (cot_hbm, cot),
+            )
+        )
+    ]
+    for load in loads:
+        load.start()
+
     pieces = (
         (wq_hbm, wq, 0, 1024),
         (wc_hbm, wc, 0, 1024),
@@ -127,15 +173,26 @@
         (wkv_hbm, wkv, 1536, 1536),
         (wa_hbm, wa, 0, 1024),
     )
+    pos_x = (x + core) % 2
+    pos_z = (z + core) % 2
+    mate_x = z * 8 + ((x + 5 - 2 * pos_x) % 4) * 2 + core
+    mate_z = ((z + 9 - 2 * pos_z) % 8) * 8 + x * 2 + core
+    quarter = core * 128 + pos_x * 64 + pos_z * 32
+    spans = (
+        (quarter, 32, None),
+        (quarter, 32, mate_z),
+        (core * 128 + pos_x * 64, 64, mate_x),
+        (core * 128, 128, sib),
+    )
 
     def start_piece(i):
         hbm, full, col, width = pieces[i]
         for k in range(1, 4):
             push(
-                hbm.at[pl.ds(mult(core * 128, 128), 128), pl.ds(col, width)],
-                full.at[pl.ds(mult(y * 256 + core * 128, 128), 128), pl.ds(col, width)],
-                w_send.at[i],
-                w_recv.at[i, k - 1],
+                hbm.at[pl.ds(mult(quarter, 32), 32), pl.ds(col, width)],
+                full.at[pl.ds(mult(y * 256 + quarter, 32), 32), pl.ds(col, width)],
+                w_send.at[i, 0],
+                w_recv.at[i, 0],
                 sp,
                 (y + k) % 4,
             )
@@ -148,26 +205,31 @@
             local_sem.at[i],
         )
 
-    def forward_piece(i):
+    def arrive(i, stage):
         hbm, full, col, width = pieces[i]
+        rows = (96, 96, 192, 384)[stage]
+        await_bytes(full.at[pl.ds(0, rows), pl.ds(col, width)], w_recv.at[i, stage])
+
+    def advance(i, stage):
+        hbm, full, col, width = pieces[i]
+        arrive(i, stage - 1)
+        first, count, mate = spans[stage]
         for k in range(1, 4):
             rows = full.at[
-                pl.ds(mult(((y - k + 4) % 4) * 256 + core * 128, 128), 128), pl.ds(col, width)
+                pl.ds(mult(((y + k) % 4) * 256 + first, 32), count), pl.ds(col, width)
             ]
-            await_bytes(rows, w_recv.at[i, k - 1])
-            push(rows, rows, f_send.at[i], f_recv.at[i], sib, y)
+            push(rows, rows, w_send.at[i, stage], w_recv.at[i, stage], mate, y)
 
     def finish_piece(i):
-        hbm, full, col, width = pieces[i]
-        await_bytes(full.at[pl.ds(0, 384), pl.ds(col, width)], f_recv.at[i])
+        arrive(i, 3)
         own_piece(i).wait()
 
     def drain_piece(i):
         hbm, full, col, width = pieces[i]
-        await_bytes(full.at[pl.ds(0, 384), pl.ds(col, width)], w_send.at[i])
-        await_bytes(full.at[pl.ds(0, 384), pl.ds(col, width)], f_send.at[i])
-
-    start_piece(0)
+        for stage in range(4):
+            rows = (96, 96, 192, 384)[stage]
+            await_bytes(full.at[pl.ds(0, rows), pl.ds(col, width)], w_send.at[i, stage])
+
     for i in range(5):
         own_piece(i).start()
     wi_copy = pltpu.make_async_copy(
@@ -179,11 +241,49 @@
     wi_copy.start()
     wo_copy.start()
 
+    loads[0].wait()
+    loads[1].wait()
+    line = lax.broadcasted_iota(jnp.int32, (96, 96), 0)
+    lane = lax.broadcasted_iota(jnp.int32, (96, 96), 1)
+
+    def upright(row):
+        return jnp.sum(jnp.where(line == lane, row, 0), axis=1, keepdims=True)
+
+    row_across = route[...]
+    row_down = upright(row_across)
+    patch_across = patch[...] + 1
+    same = row_across == row_down
+    rank_across = jnp.sum(jnp.where(same & (line < lane), 1, 0), axis=0, keepdims=True)
+    rank_down = jnp.sum(jnp.where(same & (lane < line), 1, 0), axis=1, keepdims=True)
+    slot_across = row_across * 3 + rank_across
+    slot_down = row_down * 3 + rank_down
+    hit = slot_down == lax.broadcasted_iota(jnp.int32, (96, 256), 1)
+    index_row[...] = jnp.sum(
+        jnp.where(hit, lax.broadcasted_iota(jnp.int32, (96, 256), 0), 0), axis=0, keepdims=True
+    )
+    index_copy = pltpu.make_async_copy(index_row, src_index, local_sem.at[12])
+    index_copy.start()
+    lanes = lax.broadcasted_iota(jnp.int32, (64, 128), 1)
+    found_patch = jnp.zeros((64, 128), jnp.int32)
+    for r in range(3):
+        mine = slot_across == lax.broadcasted_iota(jnp.int32, (64, 96), 0) * 3 + r
+        value = jnp.sum(jnp.where(mine, patch_across, 0), axis=1, keepdims=True) - 1
+        found_patch = jnp.where(lanes == r, value, found_patch)
+    slot_patch[...] = found_patch.astype(F32).reshape(64, 1, 128)
+
+    loads[2].wait()
+    for n in range(16):
+        pairs_wide[pl.ds(n, 96, stride=16), :] = pairs[:, n * 128 : (n + 1) * 128].astype(F32)
+    pairs_tiles[...] = pairs_wide[...].reshape(96, 16, 128).astype(BF)
+    index_copy.wait()
+
     def place(s, carry):
-        obs_send[s] = pairs[src_index[s]]
+        obs_send[s] = pairs_tiles[src_index[0, s]]
         return carry
 
     lax.fori_loop(0, 192, place, 0, unroll=8)
+    pl.semaphore_wait(barrier, 88)
+    start_piece(0)
 
     def send_obs(k, carry):
         to = (sp + k) % 64
@@ -199,9 +299,10 @@
         return carry
 
     lax.fori_loop(1, 64, send_obs, 0)
+    for i in range(1, 5):
+        start_piece(i)
     obs_recv[pl.ds(sp * 3, 3)] = obs_send[pl.ds(sp * 3, 3)]
     patch_recv[sp] = slot_patch[sp]
-    start_piece(1)
 
     def share_start(j, source, full):
         rows = full.at[pl.ds(mult(part * 128, 128), 128), :]
@@ -230,14 +331,17 @@
         await_bytes(full.at[pl.ds(0, 512), :], gather_send.at[j])
         await_bytes(full.at[pl.ds(0, 384), :], share_send.at[j])
 
-    start_piece(2)
-    share_start(0, cot, cot_all)
+    loads[3].wait()
+    loads[4].wait()
     cot_all[pl.ds(mult(part * 128, 128), 128), :] = cot[...]
-    start_piece(3)
-    start_piece(4)
 
     normed = normalize(tokens[...]).astype(BF)
-    forward_piece(0)
+    advance(0, 1)
+    advance(0, 2)
+    advance(1, 1)
+    advance(0, 3)
+    advance(1, 2)
+    advance(2, 1)
     finish_piece(0)
 
     def columns(count, width, source, weight, target, offset):
@@ -249,9 +353,16 @@
         lax.fori_loop(0, count, step, 0)
 
     columns(4, 256, normed, wq, queries, 0)
+    advance(1, 3)
+    advance(2, 2)
+    advance(3, 1)
 
     await_bytes(obs_recv.at[pl.ds(0, 189)], bulk_recv.at[0])
     await_bytes(patch_recv.at[pl.ds(0, 63)], bulk_recv.at[1])
+    advance(2, 3)
+    advance(3, 2)
+    advance(4, 1)
+    share_start(0, cot, cot_all)
     obs_wide[...] = obs_recv[...].astype(F32).reshape(3072, 128)
     patches = patch_recv[...].reshape(64, 128)
     slot_lane = lax.broadcasted_iota(jnp.int32, (64, 192), 1)
@@ -285,7 +396,8 @@
 
     lax.fori_loop(0, 8, cross_pair, 0)
 
-    forward_piece(1)
+    advance(3, 3)
+    advance(4, 2)
     finish_piece(1)
 
     def cross_out(n, carry):
@@ -297,7 +409,6 @@
 
     lax.fori_loop(0, 4, cross_out, 0)
     normed_axial = normalize(after_cross[...]).astype(BF)
-    forward_piece(2)
     finish_piece(2)
     columns(6, 256, normed_axial, wkv, axial, 0)
 
@@ -320,7 +431,7 @@
 
     share_forward(0, cot_all)
 
-    forward_piece(3)
+    advance(4, 3)
     finish_piece(3)
     columns(6, 256, normed_axial, wkv, axial, 1536)
 
@@ -384,7 +495,6 @@
 
     lax.fori_loop(1, 32, send_back, 0)
     lat_context[home] = lat_out[chip]
-    forward_piece(4)
     finish_piece(4)
     await_bytes(lat_out.at[pl.ds(0, 31)], bulk_recv.at[4])
 
@@ -420,10 +530,18 @@
 
     lax.fori_loop(0, 4, ff_rows, 0)
 
+    down = lax.broadcasted_iota(jnp.int32, (128, 128), 0)
+    across = lax.broadcasted_iota(jnp.int32, (128, 128), 1)
+    turn = (across == ((down % 32) // 4) * 16 + (down // 32) * 4 + down % 4).astype(F32).astype(BF)
+
     def grad_cols(n, carry):
         cols = pl.ds(mult(n * 256, 256), 256)
         gout_send[:, cols] = dot(hidden_t[...], cot_all[:, cols]).astype(BF)
-        gin_send[cols, :] = dot(pre_grad_t[...], normed_all[:, cols]).astype(BF).T
+        grad = dot(pre_grad_t[...], normed_all[:, cols]).astype(BF)
+        for half in range(2):
+            gin_send[pl.ds(mult(n * 256 + half * 128, 128), 128), :] = dot_t(
+                turn, grad[:, half * 128 : half * 128 + 128]
+            ).astype(BF)
         return carry
 
     lax.fori_loop(0, 4, grad_cols, 0)
@@ -478,60 +596,46 @@
     for n in range(2):
         fin_out_send[n] = sum_out[n * 8 : n * 8 + 8]
 
+    fin_in_recv[part] = fin_in_send[part]
+    for k in range(1, 8):
+        n = (part + k) % 8
+        push(
+            fin_in_send.at[n], fin_in_recv.at[part], last_send.at[0], last_in.at[0], z * 8 + n, y
+        )
+    to_sp = part * 8 + z
+    odd = y % 2
+    push(
+        fin_out_send.at[1 - odd],
+        fin_out_recv.at[odd],
+        last_send.at[1],
+        last_out.at[0],
+        to_sp,
+        y + 1 - 2 * odd,
+    )
+
+    @pl.when(part == z)
+    def _():
+        fin_out_recv[odd] = fin_out_send[odd]
+
+    @pl.when(part != z)
+    def _():
+        push(
+            fin_out_send.at[odd],
+            fin_out_recv.at[odd],
+            last_send.at[2],
+            last_out.at[1],
+            to_sp,
+            y,
+        )
+        await_bytes(fin_out_recv.at[0], last_out.at[1])
+        await_bytes(fin_out_send.at[0], last_send.at[2])
+
+    await_bytes(fin_out_recv.at[0], last_out.at[0])
+    for n in range(2):
+        out_out[:, n * 512 : (n + 1) * 512] = fin_out_recv[n]
+    await_bytes(fin_in_recv.at[pl.ds(0, 7)], last_in.at[0])
     for n in range(8):
-        to_sp, to_dp = z * 8 + y * 2 + n // 4, n % 4
-        here = (to_sp == sp) & (to_dp == y)
-
-        @pl.when(here)
-        def _():
-            fin_in_recv[part] = fin_in_send[n]
-
-        @pl.when(jnp.logical_not(here))
-        def _():
-            push(
-                fin_in_send.at[n],
-                fin_in_recv.at[part],
-                last_send.at[n],
-                last_in.at[part],
-                to_sp,
-                to_dp,
-            )
-
-    for n in range(2):
-        to_sp, to_dp = part * 8 + z, (y // 2) * 2 + n
-        here = (to_sp == sp) & (to_dp == y)
-
-        @pl.when(here)
-        def _():
-            fin_out_recv[y % 2] = fin_out_send[n]
-
-        @pl.when(jnp.logical_not(here))
-        def _():
-            push(
-                fin_out_send.at[n],
-                fin_out_recv.at[y % 2],
-                last_send.at[8 + n],
-                last_out.at[y % 2],
-                to_sp,
-                to_dp,
-            )
-
-    for n in range(8):
-        from_sp, from_dp = z * 8 + n, part // 2
-
-        @pl.when(jnp.logical_not((from_sp == sp) & (from_dp == y)))
-        def _():
-            await_bytes(fin_in_recv.at[n], last_in.at[n])
-
         out_in[:, n * 256 : (n + 1) * 256] = fin_in_recv[n]
-    for n in range(2):
-        from_sp, from_dp = part * 8 + z, (y // 2) * 2 + n
-
-        @pl.when(jnp.logical_not((from_sp == sp) & (from_dp == y)))
-        def _():
-            await_bytes(fin_out_recv.at[n], last_out.at[n])
-
-        out_out[:, n * 512 : (n + 1) * 512] = fin_out_recv[n]
 
     for i in range(5):
         drain_piece(i)
@@ -544,25 +648,24 @@
     await_bytes(lat_out.at[pl.ds(0, 31)], bulk_send.at[4])
     await_bytes(gin_recv.at[pl.ds(0, 31)], bulk_send.at[5])
     await_bytes(gout_recv.at[pl.ds(0, 31)], bulk_send.at[6])
-    for n in range(8):
-        to_sp, to_dp = z * 8 + y * 2 + n // 4, n % 4
-
-        @pl.when(jnp.logical_not((to_sp == sp) & (to_dp == y)))
-        def _():
-            await_bytes(fin_in_send.at[n], last_send.at[n])
-
-    for n in range(2):
-        to_sp, to_dp = part * 8 + z, (y // 2) * 2 + n
-
-        @pl.when(jnp.logical_not((to_sp == sp) & (to_dp == y)))
-        def _():
-            await_bytes(fin_out_send.at[n], last_send.at[8 + n])
+    await_bytes(fin_in_send.at[pl.ds(0, 7)], last_send.at[0])
+    await_bytes(fin_out_send.at[0], last_send.at[1])
 
 
 def scratch():
     vmem = pltpu.VMEM
     dma = pltpu.SemaphoreType.DMA
     return [
+        vmem((128, 1024), BF),
+        vmem((128, 1024), BF),
+        vmem((96, 2048), BF),
+        vmem((1, 96), jnp.int32),
+        vmem((1, 96), jnp.int32),
+        vmem((1536, 128), F32),
+        vmem((96, 16, 128), BF),
+        vmem((1, 256), jnp.int32),
+        pltpu.SMEM((1, 256), jnp.int32),
+        vmem((64, 1, 128), F32),
         vmem((1024, 1024), BF),
         vmem((1024, 1024), BF),
         vmem((1024, 3072), BF),
@@ -600,19 +703,17 @@
         vmem((8, 4, 256), F32),
         vmem((2, 8, 512), F32),
         vmem((2, 8, 512), F32),
-        dma((7,)),
-        dma((5,)),
-        dma((5, 3)),
-        dma((5,)),
-        dma((5,)),
+        dma((13,)),
+        dma((5, 4)),
+        dma((5, 4)),
         dma((2,)),
         dma((2, 4)),
         dma((2,)),
         dma((2,)),
         dma((7,)),
         dma((7,)),
-        dma((10,)),
-        dma((8,)),
+        dma((3,)),
+        dma((1,)),
         dma((2,)),
     ]
 
@@ -630,34 +731,26 @@
     w_in,
     w_out,
 ):
-    row = obs_route.reshape(96)
-    order = jnp.arange(96, dtype=jnp.int32)
-    earlier = (row[:, None] == row[None, :]) & (order[None, :] < order[:, None])
-    slot = row * 3 + jnp.sum(earlier.astype(jnp.int32), axis=1)
-    hit = slot[None, :] == jnp.arange(192, dtype=jnp.int32)[:, None]
-    src_index = jnp.sum(jnp.where(hit, order[None, :], 0), axis=1)
-    patch = jnp.sum(jnp.where(hit, obs_patch.reshape(1, 96) + 1, 0), axis=1) - 1
-    slot_patch = jnp.pad(patch.astype(F32).reshape(64, 1, 3), ((0, 0), (0, 0), (0, 125)))
     vmem = pl.BlockSpec(memory_space=pltpu.VMEM)
-    hbm = pl.BlockSpec(memory_space=pl.ANY)
+    hbm = pl.BlockSpec(memory_space=pltpu.HBM)
     return pl.pallas_call(
         kernel,
         out_shape=(
             jax.ShapeDtypeStruct((4, 2048), F32),
             jax.ShapeDtypeStruct((8, 1024), F32),
         ),
-        in_specs=[pl.BlockSpec(memory_space=pltpu.SMEM)] + [vmem] * 4 + [hbm] * 6,
+        in_specs=[hbm] * 11,
         out_specs=(vmem, vmem),
         scratch_shapes=scratch(),
         compiler_params=pltpu.CompilerParams(
-            has_side_effects=True, vmem_limit_bytes=50 * 1024 * 1024
+            collective_id=0, has_side_effects=True, vmem_limit_bytes=62 * 1024 * 1024
         ),
     )(
-        src_index,
         grid_tokens.reshape(128, 1024),
         cotangent.reshape(128, 1024),
-        obs_pairs.reshape(96, 16, 128),
-        slot_patch,
+        obs_pairs.reshape(96, 2048),
+        obs_route.reshape(1, 96),
+        obs_patch.reshape(1, 96),
         w_query,
         w_cross_out,
         w_qkv,

time: 160 us -> 157 us (0.981)
  Pallas kernels: 148 us -> 153 us
  local copies, waits for them, and re-layouts: 7.47 us -> 2.75 us
  other arithmetic: 2.4 us -> 0 us
    pallas_call x1, Pallas kernels: 148 us -> 153 us  [local(): pl.pallas_call(kernel, out_shape=(jax.ShapeDtypeStruct((4, 2048), F32), j...]
    unnamed x13 -> x2, local copies, waits for them, and re-layouts: 7.31 us -> 2.75 us
where the time goes in v2:
time: 157 us
  Pallas kernels  153 us (97%)
  local copies, waits for them, and re-layouts  2.75 us (2%)
    pallas_call x1, Pallas kernels, local(): pl.pallas_call(kernel, out_shape=(jax.ShapeDtypeStruct((4, 2048), F32), j...  153 us

profile of v2, /device:TPU:2, one launch (start us, length us, event | category | flops | bytes accessed | tf_op | source)
XLA Modules:
  0.0 156.7 jit_solution(12573974358779929553)
XLA Ops:
  0.6 153.3 %shard_map.122 = (f32[4,2048]{1,0:T(4,128)}, f32[8,1024]{1,0:T(8,128)}) custom-call(bf16[128,1024]{1,0:T(8,128)(2,1)} %bitcast.6, bf16[128,1024]{1,0:T(8,128)(2,1)} %bitcast.7, bf16[96,2048]{1,0:T(8,128)(2,1)} %bitcast.5, s32[1,96]{1,0:T(1,128)} %bitcast.8, s32[1,96]{1,0:T(1,128)} %bitcast.9, bf16[256,1024]{1,0:T(8,128)(2,1)} %wq_hbm.1, ...), custom_call_target="tpu_custom_call" | custom-call | tf_op jit(solution)/shard_map/pallas_call | solution.py:736
  154.0 1.4 copy.15
  155.3 1.4 copy.16

commit v3 on v2

--- a/solution.py
+++ b/solution.py
@@ -94,6 +94,7 @@
     lat_out,
     lat_context,
     lon_context,
+    axial_sum,
     normed_all,
     cot_all,
     hidden_t,
@@ -167,30 +168,43 @@
         load.start()
 
     pieces = (
-        (wq_hbm, wq, 0, 1024),
-        (wc_hbm, wc, 0, 1024),
-        (wkv_hbm, wkv, 0, 1536),
-        (wkv_hbm, wkv, 1536, 1536),
-        (wa_hbm, wa, 0, 1024),
+        (wq_hbm, wq, 0, 1024, "x"),
+        (wc_hbm, wc, 0, 1024, "x"),
+        (wkv_hbm, wkv, 0, 1536, "xz"),
+        (wkv_hbm, wkv, 1536, 1536, "zx"),
+        (wa_hbm, wa, 0, 1024, "x"),
     )
-    pos_x = (x + core) % 2
-    pos_z = (z + core) % 2
-    mate_x = z * 8 + ((x + 5 - 2 * pos_x) % 4) * 2 + core
-    mate_z = ((z + 9 - 2 * pos_z) % 8) * 8 + x * 2 + core
-    quarter = core * 128 + pos_x * 64 + pos_z * 32
-    spans = (
-        (quarter, 32, None),
-        (quarter, 32, mate_z),
-        (core * 128 + pos_x * 64, 64, mate_x),
-        (core * 128, 128, sib),
-    )
+    place_of = {"x": (x + core) % 2, "z": (z + core) % 2}
+    mate_of = {
+        "x": z * 8 + ((x + 5 - 2 * place_of["x"]) % 4) * 2 + core,
+        "z": ((z + 9 - 2 * place_of["z"]) % 8) * 8 + x * 2 + core,
+    }
+
+    def spans(plan):
+        rows = 128 >> len(plan)
+        first = core * 128
+        for n, axis in enumerate(plan):
+            first += place_of[axis] * (rows << n)
+        made = [(first, rows, None)]
+        for n, axis in enumerate(plan):
+            made.append((first, rows << n, mate_of[axis]))
+            first -= place_of[axis] * (rows << n)
+        made.append((core * 128, 128, sib))
+        return made
+
+    stages = [spans(piece[4]) for piece in pieces]
+
+    def landing(i, stage):
+        full, col, width = pieces[i][1:4]
+        return full.at[pl.ds(0, 3 * stages[i][stage][1]), pl.ds(col, width)]
 
     def start_piece(i):
-        hbm, full, col, width = pieces[i]
+        hbm, full, col, width, _ = pieces[i]
+        first, rows, _ = stages[i][0]
         for k in range(1, 4):
             push(
-                hbm.at[pl.ds(mult(quarter, 32), 32), pl.ds(col, width)],
-                full.at[pl.ds(mult(y * 256 + quarter, 32), 32), pl.ds(col, width)],
+                hbm.at[pl.ds(mult(first, 32), rows), pl.ds(col, width)],
+                full.at[pl.ds(mult(y * 256 + first, 32), rows), pl.ds(col, width)],
                 w_send.at[i, 0],
                 w_recv.at[i, 0],
                 sp,
@@ -198,37 +212,31 @@
             )
 
     def own_piece(i):
-        hbm, full, col, width = pieces[i]
+        hbm, full, col, width, _ = pieces[i]
         return pltpu.make_async_copy(
             hbm.at[:, pl.ds(col, width)],
             full.at[pl.ds(mult(y * 256, 256), 256), pl.ds(col, width)],
             local_sem.at[i],
         )
 
-    def arrive(i, stage):
-        hbm, full, col, width = pieces[i]
-        rows = (96, 96, 192, 384)[stage]
-        await_bytes(full.at[pl.ds(0, rows), pl.ds(col, width)], w_recv.at[i, stage])
-
     def advance(i, stage):
-        hbm, full, col, width = pieces[i]
-        arrive(i, stage - 1)
-        first, count, mate = spans[stage]
+        full, col, width = pieces[i][1:4]
+        await_bytes(landing(i, stage - 1), w_recv.at[i, stage - 1])
+        first, rows, mate = stages[i][stage]
         for k in range(1, 4):
-            rows = full.at[
-                pl.ds(mult(((y + k) % 4) * 256 + first, 32), count), pl.ds(col, width)
+            part_rows = full.at[
+                pl.ds(mult(((y + k) % 4) * 256 + first, 32), rows), pl.ds(col, width)
             ]
-            push(rows, rows, w_send.at[i, stage], w_recv.at[i, stage], mate, y)
+            push(part_rows, part_rows, w_send.at[i, stage], w_recv.at[i, stage], mate, y)
 
     def finish_piece(i):
-        arrive(i, 3)
+        last = len(stages[i]) - 1
+        await_bytes(landing(i, last), w_recv.at[i, last])
         own_piece(i).wait()
 
     def drain_piece(i):
-        hbm, full, col, width = pieces[i]
-        for stage in range(4):
-            rows = (96, 96, 192, 384)[stage]
-            await_bytes(full.at[pl.ds(0, rows), pl.ds(col, width)], w_send.at[i, stage])
+        for stage in range(len(stages[i])):
+            await_bytes(landing(i, stage), w_send.at[i, stage])
 
     for i in range(5):
         own_piece(i).start()
@@ -299,8 +307,7 @@
         return carry
 
     lax.fori_loop(1, 64, send_obs, 0)
-    for i in range(1, 5):
-        start_piece(i)
+    start_piece(1)
     obs_recv[pl.ds(sp * 3, 3)] = obs_send[pl.ds(sp * 3, 3)]
     patch_recv[sp] = slot_patch[sp]
 
@@ -317,15 +324,14 @@
                 y,
             )
 
-    def share_forward(j, full):
-        for k in range(1, 4):
-            rows = full.at[pl.ds(mult((((x - k + 4) % 4) * 2 + core) * 128, 128), 128), :]
-            await_bytes(rows, gather_recv.at[j, k])
-            push(rows, rows, share_send.at[j], share_recv.at[j], sib, y)
-
-    def share_finish(j, full):
-        await_bytes(full.at[pl.ds(0, 128), :], gather_recv.at[j, 0])
-        await_bytes(full.at[pl.ds(0, 384), :], share_recv.at[j])
+    def from_chip(full, k, cores):
+        first = ((x - k + 4) % 4) * 256 + (core * 128 if cores == 1 else 0)
+        return full.at[pl.ds(mult(first, 128), 128 * cores), :]
+
+    def share_forward(j, full, k):
+        rows = from_chip(full, k, 1)
+        await_bytes(rows, gather_recv.at[j, k])
+        push(rows, rows, share_send.at[j], share_recv.at[j, k], sib, y)
 
     def share_drain(j, full):
         await_bytes(full.at[pl.ds(0, 512), :], gather_send.at[j])
@@ -337,11 +343,10 @@
 
     normed = normalize(tokens[...]).astype(BF)
     advance(0, 1)
+    start_piece(2)
+    advance(1, 1)
+    start_piece(3)
     advance(0, 2)
-    advance(1, 1)
-    advance(0, 3)
-    advance(1, 2)
-    advance(2, 1)
     finish_piece(0)
 
     def columns(count, width, source, weight, target, offset):
@@ -353,16 +358,17 @@
         lax.fori_loop(0, count, step, 0)
 
     columns(4, 256, normed, wq, queries, 0)
-    advance(1, 3)
+    advance(1, 2)
+    advance(2, 1)
+    start_piece(4)
+    advance(3, 1)
     advance(2, 2)
-    advance(3, 1)
+    advance(4, 1)
 
     await_bytes(obs_recv.at[pl.ds(0, 189)], bulk_recv.at[0])
     await_bytes(patch_recv.at[pl.ds(0, 63)], bulk_recv.at[1])
     advance(2, 3)
     advance(3, 2)
-    advance(4, 1)
-    share_start(0, cot, cot_all)
     obs_wide[...] = obs_recv[...].astype(F32).reshape(3072, 128)
     patches = patch_recv[...].reshape(64, 128)
     slot_lane = lax.broadcasted_iota(jnp.int32, (64, 192), 1)
@@ -394,7 +400,7 @@
         context[:, cols] = jnp.where(low, found[0], found[1]).astype(BF)
         return carry
 
-    lax.fori_loop(0, 8, cross_pair, 0)
+    lax.fori_loop(0, 8, cross_pair, 0, unroll=4)
 
     advance(3, 3)
     advance(4, 2)
@@ -429,9 +435,8 @@
     lax.fori_loop(1, 32, send_lat, 0)
     lat_own[chip] = axial[pl.ds(mult(cell_at * 16, 16), 16), pl.ds(mult(group_at * 384, 128), 384)]
 
-    share_forward(0, cot_all)
-
-    advance(4, 3)
+    share_start(0, cot, cot_all)
+
     finish_piece(3)
     columns(6, 256, normed_axial, wkv, axial, 1536)
 
@@ -453,7 +458,7 @@
     lat_kv = lat_own.at[:, :, pl.ds(128, 256)]
     await_bytes(lat_own.at[pl.ds(0, 31)], bulk_recv.at[2])
     push(lat_kv, lat_sib, bulk_send.at[3], bulk_recv.at[3], sib, y)
-    lax.fori_loop(0, 4, lon_pair, 0)
+    lax.fori_loop(0, 4, lon_pair, 0, unroll=4)
     q_wide[...] = lat_own[:, :, 0:128].astype(F32).reshape(512, 128)
     k_wide[...] = lat_own[:, :, 128:256].astype(F32).reshape(512, 128)
     v_wide[...] = lat_own[:, :, 256:384].astype(F32).reshape(512, 128)
@@ -477,7 +482,7 @@
         o_wide[rows, :] = jnp.where(low_rows, found[:32], found[32:])
         return carry
 
-    lax.fori_loop(0, 16, lat_cell, 0, unroll=4)
+    lax.fori_loop(0, 16, lat_cell, 0, unroll=8)
     lat_out[...] = o_wide[...].reshape(32, 16, 128).astype(BF)
     home = (pl.ds(mult(cell_at * 16, 16), 16), pl.ds(mult(group_at * 128, 128), 128))
 
@@ -496,30 +501,53 @@
     lax.fori_loop(1, 32, send_back, 0)
     lat_context[home] = lat_out[chip]
     finish_piece(4)
-    await_bytes(lat_out.at[pl.ds(0, 31)], bulk_recv.at[4])
-
-    mine = pl.ds(mult(part * 128, 128), 128)
-
-    def axial_out(n, carry):
+
+    def axial_lon(n, carry):
+        cols = pl.ds(mult(n * 256, 256), 256)
+        axial_sum[:, cols] = after_cross[:, cols].astype(F32) + dot(
+            lon_context[...], wa[pl.ds(512, 512), cols]
+        )
+        return carry
+
+    def axial_lat(n, carry):
         cols = pl.ds(mult(n * 256, 256), 256)
         context[:, cols] = (
-            after_cross[:, cols].astype(F32)
-            + dot(lat_context[...], wa[pl.ds(0, 512), cols])
-            + dot(lon_context[...], wa[pl.ds(512, 512), cols])
+            axial_sum[:, cols] + dot(lat_context[...], wa[pl.ds(0, 512), cols])
         ).astype(BF)
         return carry
 
-    lax.fori_loop(0, 4, axial_out, 0)
+    lax.fori_loop(0, 4, axial_lon, 0)
+    await_bytes(lat_out.at[pl.ds(0, 31)], bulk_recv.at[4])
+    lax.fori_loop(0, 4, axial_lat, 0)
+    mine = pl.ds(mult(part * 128, 128), 128)
     normed_all[mine, :] = normalize(context[...]).astype(BF)
     share_start(1, normed_all.at[mine, :], normed_all)
-    share_finish(0, cot_all)
+    for k in range(1, 4):
+        share_forward(0, cot_all, k)
+    await_bytes(cot_all.at[pl.ds(0, 128), :], gather_recv.at[0, 0])
+    for k in range(1, 4):
+        await_bytes(from_chip(cot_all, k, 1), share_recv.at[0, k])
     wi_copy.wait()
     wo_copy.wait()
-    share_forward(1, normed_all)
-    share_finish(1, normed_all)
-
-    def ff_rows(n, carry):
-        rows = pl.ds(mult(n * 256, 256), 256)
+    await_bytes(normed_all.at[pl.ds(0, 128), :], gather_recv.at[1, 0])
+
+    def ff_chip(i, carry):
+        k = jnp.where(i == 2, 3, jnp.where(i == 3, 2, i))
+
+        @pl.when(i == 1)
+        def _():
+            share_forward(1, normed_all, 1)
+            share_forward(1, normed_all, 3)
+
+        @pl.when(i == 2)
+        def _():
+            share_forward(1, normed_all, 2)
+
+        @pl.when(i > 0)
+        def _():
+            await_bytes(normed_all.at[pl.ds(0, 128), :], share_recv.at[1, k])
+
+        rows = pl.ds(mult(((x - k + 4) % 4) * 256, 256), 256)
         pre_act = dot(normed_all[rows, :], wi[...])
         hidden_grad = dot_t(cot_all[rows, :], wo[...])
         cdf = 0.5 * (1.0 + lax.erf(pre_act * ROOT_HALF))
@@ -528,7 +556,39 @@
         pre_grad_t[:, rows] = (hidden_grad * slope).astype(BF).T
         return carry
 
-    lax.fori_loop(0, 4, ff_rows, 0)
+    lax.fori_loop(0, 4, ff_chip, 0)
+
+    place_at = z * 4 + y
+
+    def in_block(to):
+        return (pl.ds(mult(to * 32, 32), 32), slice(None))
+
+    def out_block(to):
+        return (pl.ds(mult((to // 2) * 16, 16), 16), pl.ds(mult((to % 2) * 512, 512), 512))
+
+    def send_grads(source, block, received, at):
+        def one(k, carry):
+            to = (place_at + k) % 32
+            push(
+                source.at[block(to)],
+                received.at[place_at],
+                bulk_send.at[at],
+                bulk_recv.at[at],
+                (to // 4) * 8 + part,
+                to % 4,
+            )
+            return carry
+
+        lax.fori_loop(1, 32, one, 0)
+        received[place_at] = source[block(place_at)]
+
+    def grad_out_cols(n, carry):
+        cols = pl.ds(mult(n * 256, 256), 256)
+        gout_send[:, cols] = dot(hidden_t[...], cot_all[:, cols]).astype(BF)
+        return carry
+
+    lax.fori_loop(0, 4, grad_out_cols, 0)
+    send_grads(gout_send, out_block, gout_recv, 6)
 
     down = lax.broadcasted_iota(jnp.int32, (128, 128), 0)
     across = lax.broadcasted_iota(jnp.int32, (128, 128), 1)
@@ -536,7 +596,6 @@
 
     def grad_cols(n, carry):
         cols = pl.ds(mult(n * 256, 256), 256)
-        gout_send[:, cols] = dot(hidden_t[...], cot_all[:, cols]).astype(BF)
         grad = dot(pre_grad_t[...], normed_all[:, cols]).astype(BF)
         for half in range(2):
             gin_send[pl.ds(mult(n * 256 + half * 128, 128), 128), :] = dot_t(
@@ -546,51 +605,17 @@
 
     lax.fori_loop(0, 4, grad_cols, 0)
 
-    place_at = z * 4 + y
-
-    def blocks(to):
-        return (
-            (pl.ds(mult(to * 32, 32), 32), slice(None)),
-            (pl.ds(mult((to // 2) * 16, 16), 16), pl.ds(mult((to % 2) * 512, 512), 512)),
-        )
-
-    def send_grads(k, carry):
-        to = (place_at + k) % 32
-        at_in, at_out = blocks(to)
-        to_sp, to_dp = (to // 4) * 8 + part, to % 4
-        push(
-            gin_send.at[at_in],
-            gin_recv.at[place_at],
-            bulk_send.at[5],
-            bulk_recv.at[5],
-            to_sp,
-            to_dp,
-        )
-        push(
-            gout_send.at[at_out],
-            gout_recv.at[place_at],
-            bulk_send.at[6],
-            bulk_recv.at[6],
-            to_sp,
-            to_dp,
-        )
-        return carry
-
-    lax.fori_loop(1, 32, send_grads, 0)
-    at_in, at_out = blocks(place_at)
-    gin_recv[place_at] = gin_send[at_in]
-    gout_recv[place_at] = gout_send[at_out]
-    await_bytes(gin_recv.at[pl.ds(0, 31)], bulk_recv.at[5])
-    await_bytes(gout_recv.at[pl.ds(0, 31)], bulk_recv.at[6])
-
+    send_grads(gin_send, in_block, gin_recv, 5)
     def add_in(n, total):
         return total + gin_recv[n].astype(F32)
 
     def add_out(n, total):
         return total + gout_recv[n].astype(F32)
 
+    await_bytes(gout_recv.at[pl.ds(0, 31)], bulk_recv.at[6])
+    sum_out = lax.fori_loop(0, 32, add_out, jnp.zeros((16, 512), F32), unroll=4)
+    await_bytes(gin_recv.at[pl.ds(0, 31)], bulk_recv.at[5])
     sum_in = lax.fori_loop(0, 32, add_in, jnp.zeros((32, 256), F32), unroll=4)
-    sum_out = lax.fori_loop(0, 32, add_out, jnp.zeros((16, 512), F32), unroll=4)
     for n in range(8):
         fin_in_send[n] = sum_in[n * 4 : n * 4 + 4]
     for n in range(2):
@@ -691,6 +716,7 @@
         vmem((32, 16, 128), BF),
         vmem((128, 512), BF),
         vmem((128, 512), BF),
+        vmem((128, 1024), F32),
         vmem((1024, 1024), BF),
         vmem((1024, 1024), BF),
         vmem((256, 1024), BF),
@@ -709,7 +735,7 @@
         dma((2,)),
         dma((2, 4)),
         dma((2,)),
-        dma((2,)),
+        dma((2, 4)),
         dma((7,)),
         dma((7,)),
         dma((3,)),

time: 157 us -> 143 us (0.911)
  Pallas kernels: 153 us -> 140 us
    pallas_call x1, Pallas kernels: 153 us -> 140 us  [local(): pl.pallas_call(kernel, out_shape=(jax.ShapeDtypeStruct((4, 2048), F32), j...]
where the time goes in v3:
time: 143 us
  Pallas kernels  140 us (98%)
  local copies, waits for them, and re-layouts  2.75 us (2%)
    pallas_call x1, Pallas kernels, local(): pl.pallas_call(kernel, out_shape=(jax.ShapeDtypeStruct((4, 2048), F32), j...  140 us

profile of v3, /device:TPU:2, one launch (start us, length us, event | category | flops | bytes accessed | tf_op | source)
XLA Modules:
  0.0 142.9 jit_solution(13251255708791401486)
XLA Ops:
  0.6 139.6 %shard_map.122 = (f32[4,2048]{1,0:T(4,128)}, f32[8,1024]{1,0:T(8,128)}) custom-call(bf16[128,1024]{1,0:T(8,128)(2,1)} %bitcast.6, bf16[128,1024]{1,0:T(8,128)(2,1)} %bitcast.7, bf16[96,2048]{1,0:T(8,128)(2,1)} %bitcast.5, s32[1,96]{1,0:T(1,128)} %bitcast.8, s32[1,96]{1,0:T(1,128)} %bitcast.9, bf16[256,1024]{1,0:T(8,128)(2,1)} %wq_hbm.1, ...), custom_call_target="tpu_custom_call" | custom-call | tf_op jit(solution)/shard_map/pallas_call | solution.py:762
  140.2 1.4 copy.15
  141.6 1.4 copy.16

commit v4 on v3

--- a/solution.py
+++ b/solution.py
@@ -103,6 +103,10 @@
     gout_send,
     gin_recv,
     gout_recv,
+    gin_mid,
+    gout_mid,
+    gin_ends,
+    gout_ends,
     fin_in_send,
     fin_in_recv,
     fin_out_send,
@@ -119,6 +123,7 @@
     last_send,
     last_in,
     last_out,
+    entered,
 ):
     sp = lax.axis_index("sp")
     y = lax.axis_index("dp")
@@ -139,17 +144,14 @@
             device_id_type=pl.DeviceIdType.MESH,
         )
 
-    def greet_row(k, carry):
-        greet((sp + k) % 64, y)
-        return carry
-
-    def greet_member(k, carry):
-        for other in range(1, 4):
-            greet(k * 8 + part, (y + other) % 4)
-        return carry
-
-    lax.fori_loop(1, 64, greet_row, 0)
-    lax.fori_loop(0, 8, greet_member, 0)
+    def greet_line(k, carry):
+        greet(((z + k) % 8) * 8 + part, y)
+        greet(z * 8 + (part + k) % 8, y)
+        return carry
+
+    lax.fori_loop(1, 8, greet_line, 0)
+    for k in range(1, 4):
+        greet(sp, (y + k) % 4)
     greet(part * 8 + z, y + 1 - 2 * (y % 2))
 
     loads = [
@@ -279,6 +281,19 @@
         found_patch = jnp.where(lanes == r, value, found_patch)
     slot_patch[...] = found_patch.astype(F32).reshape(64, 1, 128)
 
+    pl.semaphore_wait(barrier, 18)
+
+    def greet_again(k, carry):
+        pl.semaphore_signal(
+            entered,
+            inc=1,
+            device_id={"sp": z * 8 + (part + k) % 8, "dp": y},
+            device_id_type=pl.DeviceIdType.MESH,
+        )
+        return carry
+
+    lax.fori_loop(1, 8, greet_again, 0)
+
     loads[2].wait()
     for n in range(16):
         pairs_wide[pl.ds(n, 96, stride=16), :] = pairs[:, n * 128 : (n + 1) * 128].astype(F32)
@@ -290,7 +305,7 @@
         return carry
 
     lax.fori_loop(0, 192, place, 0, unroll=8)
-    pl.semaphore_wait(barrier, 88)
+    pl.semaphore_wait(entered, 7)
     start_piece(0)
 
     def send_obs(k, carry):
@@ -558,37 +573,61 @@
 
     lax.fori_loop(0, 4, ff_chip, 0)
 
-    place_at = z * 4 + y
-
-    def in_block(to):
-        return (pl.ds(mult(to * 32, 32), 32), slice(None))
-
-    def out_block(to):
-        return (pl.ds(mult((to // 2) * 16, 16), 16), pl.ds(mult((to % 2) * 512, 512), 512))
-
-    def send_grads(source, block, received, at):
-        def one(k, carry):
-            to = (place_at + k) % 32
+    def fold(source, received, at):
+        for k in range(1, 4):
             push(
-                source.at[block(to)],
-                received.at[place_at],
+                source.at[(y + k) % 4],
+                received.at[y],
                 bulk_send.at[at],
                 bulk_recv.at[at],
-                (to // 4) * 8 + part,
-                to % 4,
+                sp,
+                (y + k) % 4,
+            )
+        received[y] = source[y]
+
+    def pass_on(received, middle, ends, at, to):
+        await_bytes(received.at[pl.ds(0, 3)], bulk_recv.at[at])
+
+        def total(n, carry):
+            found = received[0, n].astype(F32)
+            for k in range(1, 4):
+                found += received[k, n].astype(F32)
+            middle[n] = found.astype(BF)
+            return carry
+
+        lax.fori_loop(0, 8, total, 0)
+
+        def one(k, carry):
+            push(
+                middle.at[(z + k) % 8],
+                ends.at[z],
+                bulk_send.at[to],
+                bulk_recv.at[to],
+                ((z + k) % 8) * 8 + part,
+                y,
             )
             return carry
 
-        lax.fori_loop(1, 32, one, 0)
-        received[place_at] = source[block(place_at)]
+        lax.fori_loop(1, 8, one, 0)
+        ends[z] = middle[z]
+
+    def end_sum(ends, at):
+        await_bytes(ends.at[pl.ds(0, 7)], bulk_recv.at[at])
+        found = ends[0].astype(F32)
+        for n in range(1, 8):
+            found += ends[n].astype(F32)
+        return found
 
     def grad_out_cols(n, carry):
         cols = pl.ds(mult(n * 256, 256), 256)
-        gout_send[:, cols] = dot(hidden_t[...], cot_all[:, cols]).astype(BF)
+        grad = dot(hidden_t[...], cot_all[:, cols]).astype(BF)
+        inner = pl.ds(mult((n % 2) * 256, 256), 256)
+        for at in range(16):
+            gout_send[(at % 2) * 2 + n // 2, at // 2, :, inner] = grad[at * 16 : at * 16 + 16]
         return carry
 
     lax.fori_loop(0, 4, grad_out_cols, 0)
-    send_grads(gout_send, out_block, gout_recv, 6)
+    fold(gout_send, gout_recv, 6)
 
     down = lax.broadcasted_iota(jnp.int32, (128, 128), 0)
     across = lax.broadcasted_iota(jnp.int32, (128, 128), 1)
@@ -598,24 +637,18 @@
         cols = pl.ds(mult(n * 256, 256), 256)
         grad = dot(pre_grad_t[...], normed_all[:, cols]).astype(BF)
         for half in range(2):
-            gin_send[pl.ds(mult(n * 256 + half * 128, 128), 128), :] = dot_t(
-                turn, grad[:, half * 128 : half * 128 + 128]
-            ).astype(BF)
+            turned = dot_t(turn, grad[:, half * 128 : half * 128 + 128]).astype(BF)
+            for m in range(4):
+                gin_send[m, n * 2 + half] = turned[m * 32 : m * 32 + 32]
         return carry
 
     lax.fori_loop(0, 4, grad_cols, 0)
 
-    send_grads(gin_send, in_block, gin_recv, 5)
-    def add_in(n, total):
-        return total + gin_recv[n].astype(F32)
-
-    def add_out(n, total):
-        return total + gout_recv[n].astype(F32)
-
-    await_bytes(gout_recv.at[pl.ds(0, 31)], bulk_recv.at[6])
-    sum_out = lax.fori_loop(0, 32, add_out, jnp.zeros((16, 512), F32), unroll=4)
-    await_bytes(gin_recv.at[pl.ds(0, 31)], bulk_recv.at[5])
-    sum_in = lax.fori_loop(0, 32, add_in, jnp.zeros((32, 256), F32), unroll=4)
+    fold(gin_send, gin_recv, 5)
+    pass_on(gout_recv, gout_mid, gout_ends, 6, 8)
+    pass_on(gin_recv, gin_mid, gin_ends, 5, 7)
+    sum_out = end_sum(gout_ends, 8)
+    sum_in = end_sum(gin_ends, 7)
     for n in range(8):
         fin_in_send[n] = sum_in[n * 4 : n * 4 + 4]
     for n in range(2):
@@ -671,8 +704,10 @@
     await_bytes(lat_own.at[pl.ds(0, 31)], bulk_send.at[2])
     await_bytes(lat_sib, bulk_send.at[3])
     await_bytes(lat_out.at[pl.ds(0, 31)], bulk_send.at[4])
-    await_bytes(gin_recv.at[pl.ds(0, 31)], bulk_send.at[5])
-    await_bytes(gout_recv.at[pl.ds(0, 31)], bulk_send.at[6])
+    await_bytes(gin_recv.at[pl.ds(0, 3)], bulk_send.at[5])
+    await_bytes(gout_recv.at[pl.ds(0, 3)], bulk_send.at[6])
+    await_bytes(gin_ends.at[pl.ds(0, 7)], bulk_send.at[7])
+    await_bytes(gout_ends.at[pl.ds(0, 7)], bulk_send.at[8])
     await_bytes(fin_in_send.at[pl.ds(0, 7)], last_send.at[0])
     await_bytes(fin_out_send.at[0], last_send.at[1])
 
@@ -721,10 +756,14 @@
         vmem((1024, 1024), BF),
         vmem((256, 1024), BF),
         vmem((256, 1024), BF),
-        vmem((1024, 256), BF),
-        vmem((256, 1024), BF),
-        vmem((32, 32, 256), BF),
-        vmem((32, 16, 512), BF),
+        vmem((4, 8, 32, 256), BF),
+        vmem((4, 8, 16, 512), BF),
+        vmem((4, 8, 32, 256), BF),
+        vmem((4, 8, 16, 512), BF),
+        vmem((8, 32, 256), BF),
+        vmem((8, 16, 512), BF),
+        vmem((8, 32, 256), BF),
+        vmem((8, 16, 512), BF),
         vmem((8, 4, 256), F32),
         vmem((8, 4, 256), F32),
         vmem((2, 8, 512), F32),
@@ -736,11 +775,12 @@
         dma((2, 4)),
         dma((2,)),
         dma((2, 4)),
-        dma((7,)),
-        dma((7,)),
+        dma((9,)),
+        dma((9,)),
         dma((3,)),
         dma((1,)),
         dma((2,)),
+        pltpu.SemaphoreType.REGULAR,
     ]
 
 

time: 143 us -> 138 us (0.965); the launches traced: 143 us -> 135 us
  Pallas kernels: 140 us -> 132 us
    pallas_call x1, Pallas kernels: 140 us -> 132 us  [local(): pl.pallas_call(kernel, out_shape=(jax.ShapeDtypeStruct((4, 2048), F32), j...]
where the time goes in v4:
time: 138 us; the launch traced here: 135 us
  Pallas kernels  132 us (96%)
  local copies, waits for them, and re-layouts  2.75 us (2%)
    pallas_call x1, Pallas kernels, local(): pl.pallas_call(kernel, out_shape=(jax.ShapeDtypeStruct((4, 2048), F32), j...  132 us

profile of v4, /device:TPU:2, one launch (start us, length us, event | category | flops | bytes accessed | tf_op | source)
XLA Modules:
  0.0 135.3 jit_solution(254145939489877697)
XLA Ops:
  0.6 131.9 %shard_map.122 = (f32[4,2048]{1,0:T(4,128)}, f32[8,1024]{1,0:T(8,128)}) custom-call(bf16[128,1024]{1,0:T(8,128)(2,1)} %bitcast.6, bf16[128,1024]{1,0:T(8,128)(2,1)} %bitcast.7, bf16[96,2048]{1,0:T(8,128)(2,1)} %bitcast.5, s32[1,96]{1,0:T(1,128)} %bitcast.8, s32[1,96]{1,0:T(1,128)} %bitcast.9, bf16[256,1024]{1,0:T(8,128)(2,1)} %wq_hbm.1, ...), custom_call_target="tpu_custom_call" | custom-call | tf_op jit(solution)/shard_map/pallas_call | solution.py:802
  132.5 1.4 %copy.15 = f32[4,2048]{1,0:T(4,128)} copy(f32[4,2048]{1,0:T(4,128)} %get-tuple-element.4) | data formatting | bytes 65536
  133.9 1.4 %copy.16 = f32[8,1024]{1,0:T(8,128)} copy(f32[8,1024]{1,0:T(8,128)} %get-tuple-element.5) | data formatting | bytes 65536

commit v5 on v4

--- a/solution.py
+++ b/solution.py
@@ -323,6 +323,7 @@
 
     lax.fori_loop(1, 64, send_obs, 0)
     start_piece(1)
+    start_piece(2)
     obs_recv[pl.ds(sp * 3, 3)] = obs_send[pl.ds(sp * 3, 3)]
     patch_recv[sp] = slot_patch[sp]
 
@@ -358,9 +359,7 @@
 
     normed = normalize(tokens[...]).astype(BF)
     advance(0, 1)
-    start_piece(2)
     advance(1, 1)
-    start_piece(3)
     advance(0, 2)
     finish_piece(0)
 
@@ -373,17 +372,13 @@
         lax.fori_loop(0, count, step, 0)
 
     columns(4, 256, normed, wq, queries, 0)
+    advance(2, 1)
+    start_piece(3)
     advance(1, 2)
-    advance(2, 1)
-    start_piece(4)
-    advance(3, 1)
     advance(2, 2)
-    advance(4, 1)
 
     await_bytes(obs_recv.at[pl.ds(0, 189)], bulk_recv.at[0])
     await_bytes(patch_recv.at[pl.ds(0, 63)], bulk_recv.at[1])
-    advance(2, 3)
-    advance(3, 2)
     obs_wide[...] = obs_recv[...].astype(F32).reshape(3072, 128)
     patches = patch_recv[...].reshape(64, 128)
     slot_lane = lax.broadcasted_iota(jnp.int32, (64, 192), 1)
@@ -415,10 +410,19 @@
         context[:, cols] = jnp.where(low, found[0], found[1]).astype(BF)
         return carry
 
-    lax.fori_loop(0, 8, cross_pair, 0, unroll=4)
-
-    advance(3, 3)
-    advance(4, 2)
+    def cross_four(i, carry):
+        @pl.when(i == 1)
+        def _():
+            advance(2, 3)
+            advance(3, 1)
+            start_piece(4)
+
+        for g in range(4):
+            cross_pair(i * 4 + g, 0)
+        return carry
+
+    lax.fori_loop(0, 2, cross_four, 0)
+
     finish_piece(1)
 
     def cross_out(n, carry):
@@ -429,6 +433,7 @@
         return carry
 
     lax.fori_loop(0, 4, cross_out, 0)
+    advance(3, 2)
     normed_axial = normalize(after_cross[...]).astype(BF)
     finish_piece(2)
     columns(6, 256, normed_axial, wkv, axial, 0)
@@ -452,6 +457,8 @@
 
     share_start(0, cot, cot_all)
 
+    advance(4, 1)
+    advance(3, 3)
     finish_piece(3)
     columns(6, 256, normed_axial, wkv, axial, 1536)
 
@@ -474,6 +481,7 @@
     await_bytes(lat_own.at[pl.ds(0, 31)], bulk_recv.at[2])
     push(lat_kv, lat_sib, bulk_send.at[3], bulk_recv.at[3], sib, y)
     lax.fori_loop(0, 4, lon_pair, 0, unroll=4)
+    advance(4, 2)
     q_wide[...] = lat_own[:, :, 0:128].astype(F32).reshape(512, 128)
     k_wide[...] = lat_own[:, :, 128:256].astype(F32).reshape(512, 128)
     v_wide[...] = lat_own[:, :, 256:384].astype(F32).reshape(512, 128)

time: 138 us -> 144 us (1.043)
  Pallas kernels: 132 us -> 138 us
    pallas_call x1, Pallas kernels: 132 us -> 138 us  [local(): pl.pallas_call(kernel, out_shape=(jax.ShapeDtypeStruct((4, 2048), F32), j...]
where the time goes in v5:
time: 144 us; the launch traced here: 142 us
  Pallas kernels  138 us (96%)
  local copies, waits for them, and re-layouts  2.75 us (2%)
    pallas_call x1, Pallas kernels, local(): pl.pallas_call(kernel, out_shape=(jax.ShapeDtypeStruct((4, 2048), F32), j...  138 us

profile of v5, /device:TPU:2, one launch (start us, length us, event | category | flops | bytes accessed | tf_op | source)
XLA Modules:
  0.0 141.9 jit_solution(18312344194864604710)
XLA Ops:
  0.6 138.5 %shard_map.122 = (f32[4,2048]{1,0:T(4,128)}, f32[8,1024]{1,0:T(8,128)}) custom-call(bf16[128,1024]{1,0:T(8,128)(2,1)} %bitcast.6, bf16[128,1024]{1,0:T(8,128)(2,1)} %bitcast.7, bf16[96,2048]{1,0:T(8,128)(2,1)} %bitcast.5, s32[1,96]{1,0:T(1,128)} %bitcast.8, s32[1,96]{1,0:T(1,128)} %bitcast.9, bf16[256,1024]{1,0:T(8,128)(2,1)} %wq_hbm.1, ...), custom_call_target="tpu_custom_call" | custom-call | tf_op jit(solution)/shard_map/pallas_call | solution.py:810
  139.1 1.4 copy.15
  140.5 1.4 copy.16

commit v6 on v5

--- a/solution.py
+++ b/solution.py
@@ -361,6 +361,7 @@
     advance(0, 1)
     advance(1, 1)
     advance(0, 2)
+    start_piece(3)
     finish_piece(0)
 
     def columns(count, width, source, weight, target, offset):
@@ -373,7 +374,7 @@
 
     columns(4, 256, normed, wq, queries, 0)
     advance(2, 1)
-    start_piece(3)
+    start_piece(4)
     advance(1, 2)
     advance(2, 2)
 
@@ -415,7 +416,7 @@
         def _():
             advance(2, 3)
             advance(3, 1)
-            start_piece(4)
+            advance(4, 1)
 
         for g in range(4):
             cross_pair(i * 4 + g, 0)
@@ -434,6 +435,8 @@
 
     lax.fori_loop(0, 4, cross_out, 0)
     advance(3, 2)
+    advance(4, 2)
+    share_start(0, cot, cot_all)
     normed_axial = normalize(after_cross[...]).astype(BF)
     finish_piece(2)
     columns(6, 256, normed_axial, wkv, axial, 0)
@@ -455,9 +458,6 @@
     lax.fori_loop(1, 32, send_lat, 0)
     lat_own[chip] = axial[pl.ds(mult(cell_at * 16, 16), 16), pl.ds(mult(group_at * 384, 128), 384)]
 
-    share_start(0, cot, cot_all)
-
-    advance(4, 1)
     advance(3, 3)
     finish_piece(3)
     columns(6, 256, normed_axial, wkv, axial, 1536)
@@ -481,7 +481,6 @@
     await_bytes(lat_own.at[pl.ds(0, 31)], bulk_recv.at[2])
     push(lat_kv, lat_sib, bulk_send.at[3], bulk_recv.at[3], sib, y)
     lax.fori_loop(0, 4, lon_pair, 0, unroll=4)
-    advance(4, 2)
     q_wide[...] = lat_own[:, :, 0:128].astype(F32).reshape(512, 128)
     k_wide[...] = lat_own[:, :, 128:256].astype(F32).reshape(512, 128)
     v_wide[...] = lat_own[:, :, 256:384].astype(F32).reshape(512, 128)
@@ -539,14 +538,14 @@
         ).astype(BF)
         return carry
 
+    for k in range(1, 4):
+        share_forward(0, cot_all, k)
     lax.fori_loop(0, 4, axial_lon, 0)
     await_bytes(lat_out.at[pl.ds(0, 31)], bulk_recv.at[4])
     lax.fori_loop(0, 4, axial_lat, 0)
     mine = pl.ds(mult(part * 128, 128), 128)
     normed_all[mine, :] = normalize(context[...]).astype(BF)
     share_start(1, normed_all.at[mine, :], normed_all)
-    for k in range(1, 4):
-        share_forward(0, cot_all, k)
     await_bytes(cot_all.at[pl.ds(0, 128), :], gather_recv.at[0, 0])
     for k in range(1, 4):
         await_bytes(from_chip(cot_all, k, 1), share_recv.at[0, k])

time: 144 us -> 142 us (0.986)
    pallas_call x1, Pallas kernels: 138 us -> 137 us  [local(): pl.pallas_call(kernel, out_shape=(jax.ShapeDtypeStruct((4, 2048), F32), j...]
where the time goes in v6:
time: 142 us; the launch traced here: 140 us
  Pallas kernels  137 us (96%)
  local copies, waits for them, and re-layouts  2.75 us (2%)
    pallas_call x1, Pallas kernels, local(): pl.pallas_call(kernel, out_shape=(jax.ShapeDtypeStruct((4, 2048), F32), j...  137 us

profile of v6, /device:TPU:2, one launch (start us, length us, event | category | flops | bytes accessed | tf_op | source)
XLA Modules:
  0.0 140.0 jit_solution(12947125641155669149)
XLA Ops:
  0.6 136.6 %shard_map.122 = (f32[4,2048]{1,0:T(4,128)}, f32[8,1024]{1,0:T(8,128)}) custom-call(bf16[128,1024]{1,0:T(8,128)(2,1)} %bitcast.6, bf16[128,1024]{1,0:T(8,128)(2,1)} %bitcast.7, bf16[96,2048]{1,0:T(8,128)(2,1)} %bitcast.5, s32[1,96]{1,0:T(1,128)} %bitcast.8, s32[1,96]{1,0:T(1,128)} %bitcast.9, bf16[256,1024]{1,0:T(8,128)(2,1)} %wq_hbm.1, ...), custom_call_target="tpu_custom_call" | custom-call | tf_op jit(solution)/shard_map/pallas_call | solution.py:809
  137.2 1.4 copy.15
  138.6 1.4 copy.16

commit v7 on v6

--- a/solution.py
+++ b/solution.py
@@ -107,6 +107,10 @@
     gout_mid,
     gin_ends,
     gout_ends,
+    gin_right,
+    right_recv,
+    right_mid,
+    right_ends,
     fin_in_send,
     fin_in_recv,
     fin_out_send,
@@ -436,7 +440,6 @@
     lax.fori_loop(0, 4, cross_out, 0)
     advance(3, 2)
     advance(4, 2)
-    share_start(0, cot, cot_all)
     normed_axial = normalize(after_cross[...]).astype(BF)
     finish_piece(2)
     columns(6, 256, normed_axial, wkv, axial, 0)
@@ -479,6 +482,7 @@
 
     lat_kv = lat_own.at[:, :, pl.ds(128, 256)]
     await_bytes(lat_own.at[pl.ds(0, 31)], bulk_recv.at[2])
+    share_start(0, cot, cot_all)
     push(lat_kv, lat_sib, bulk_send.at[3], bulk_recv.at[3], sib, y)
     lax.fori_loop(0, 4, lon_pair, 0, unroll=4)
     q_wide[...] = lat_own[:, :, 0:128].astype(F32).reshape(512, 128)
@@ -538,14 +542,14 @@
         ).astype(BF)
         return carry
 
-    for k in range(1, 4):
-        share_forward(0, cot_all, k)
     lax.fori_loop(0, 4, axial_lon, 0)
     await_bytes(lat_out.at[pl.ds(0, 31)], bulk_recv.at[4])
     lax.fori_loop(0, 4, axial_lat, 0)
     mine = pl.ds(mult(part * 128, 128), 128)
     normed_all[mine, :] = normalize(context[...]).astype(BF)
     share_start(1, normed_all.at[mine, :], normed_all)
+    for k in range(1, 4):
+        share_forward(0, cot_all, k)
     await_bytes(cot_all.at[pl.ds(0, 128), :], gather_recv.at[0, 0])
     for k in range(1, 4):
         await_bytes(from_chip(cot_all, k, 1), share_recv.at[0, k])
@@ -579,6 +583,36 @@
         return carry
 
     lax.fori_loop(0, 4, ff_chip, 0)
+
+    def fold_line(source, received, at):
+        for k in range(1, 8):
+            push(
+                source.at[(z + k) % 8],
+                received.at[z],
+                bulk_send.at[at],
+                bulk_recv.at[at],
+                ((z + k) % 8) * 8 + part,
+                y,
+            )
+        received[z] = source[z]
+
+    def pass_across(received, middle, ends, at, to):
+        await_bytes(received.at[pl.ds(0, 7)], bulk_recv.at[at])
+        for m in range(4):
+            found = received[0, m].astype(F32)
+            for k in range(1, 8):
+                found += received[k, m].astype(F32)
+            middle[m] = found.astype(BF)
+        for k in range(1, 4):
+            push(
+                middle.at[(y + k) % 4],
+                ends.at[y],
+                bulk_send.at[to],
+                bulk_recv.at[to],
+                sp,
+                (y + k) % 4,
+            )
+        ends[y] = middle[y]
 
     def fold(source, received, at):
         for k in range(1, 4):
@@ -618,10 +652,10 @@
         lax.fori_loop(1, 8, one, 0)
         ends[z] = middle[z]
 
-    def end_sum(ends, at):
-        await_bytes(ends.at[pl.ds(0, 7)], bulk_recv.at[at])
+    def end_sum(ends, at, count):
+        await_bytes(ends.at[pl.ds(0, count - 1)], bulk_recv.at[at])
         found = ends[0].astype(F32)
-        for n in range(1, 8):
+        for n in range(1, count):
             found += ends[n].astype(F32)
         return found
 
@@ -646,18 +680,23 @@
         for half in range(2):
             turned = dot_t(turn, grad[:, half * 128 : half * 128 + 128]).astype(BF)
             for m in range(4):
-                gin_send[m, n * 2 + half] = turned[m * 32 : m * 32 + 32]
+                gin_send[m, n * 2 + half] = turned[m * 32 : m * 32 + 32, :128]
+                gin_right[n * 2 + half, m] = turned[m * 32 : m * 32 + 32, 128:]
         return carry
 
     lax.fori_loop(0, 4, grad_cols, 0)
 
+    fold_line(gin_right, right_recv, 9)
     fold(gin_send, gin_recv, 5)
     pass_on(gout_recv, gout_mid, gout_ends, 6, 8)
     pass_on(gin_recv, gin_mid, gin_ends, 5, 7)
-    sum_out = end_sum(gout_ends, 8)
-    sum_in = end_sum(gin_ends, 7)
+    pass_across(right_recv, right_mid, right_ends, 9, 10)
+    sum_out = end_sum(gout_ends, 8, 8)
+    sum_in = end_sum(gin_ends, 7, 8)
+    sum_right = end_sum(right_ends, 10, 4)
     for n in range(8):
-        fin_in_send[n] = sum_in[n * 4 : n * 4 + 4]
+        fin_in_send[n, :, 0:128] = sum_in[n * 4 : n * 4 + 4]
+        fin_in_send[n, :, 128:256] = sum_right[n * 4 : n * 4 + 4]
     for n in range(2):
         fin_out_send[n] = sum_out[n * 8 : n * 8 + 8]
 
@@ -715,6 +754,8 @@
     await_bytes(gout_recv.at[pl.ds(0, 3)], bulk_send.at[6])
     await_bytes(gin_ends.at[pl.ds(0, 7)], bulk_send.at[7])
     await_bytes(gout_ends.at[pl.ds(0, 7)], bulk_send.at[8])
+    await_bytes(right_recv.at[pl.ds(0, 7)], bulk_send.at[9])
+    await_bytes(right_ends.at[pl.ds(0, 3)], bulk_send.at[10])
     await_bytes(fin_in_send.at[pl.ds(0, 7)], last_send.at[0])
     await_bytes(fin_out_send.at[0], last_send.at[1])
 
@@ -763,14 +804,18 @@
         vmem((1024, 1024), BF),
         vmem((256, 1024), BF),
         vmem((256, 1024), BF),
-        vmem((4, 8, 32, 256), BF),
+        vmem((4, 8, 32, 128), BF),
         vmem((4, 8, 16, 512), BF),
-        vmem((4, 8, 32, 256), BF),
+        vmem((4, 8, 32, 128), BF),
         vmem((4, 8, 16, 512), BF),
-        vmem((8, 32, 256), BF),
+        vmem((8, 32, 128), BF),
         vmem((8, 16, 512), BF),
-        vmem((8, 32, 256), BF),
+        vmem((8, 32, 128), BF),
         vmem((8, 16, 512), BF),
+        vmem((8, 4, 32, 128), BF),
+        vmem((8, 4, 32, 128), BF),
+        vmem((4, 32, 128), BF),
+        vmem((4, 32, 128), BF),
         vmem((8, 4, 256), F32),
         vmem((8, 4, 256), F32),
         vmem((2, 8, 512), F32),
@@ -782,8 +827,8 @@
         dma((2, 4)),
         dma((2,)),
         dma((2, 4)),
-        dma((9,)),
-        dma((9,)),
+        dma((11,)),
+        dma((11,)),
         dma((3,)),
         dma((1,)),
         dma((2,)),

time: 142 us -> 131 us (0.923)
  Pallas kernels: 137 us -> 126 us
    pallas_call x1, Pallas kernels: 137 us -> 126 us  [local(): pl.pallas_call(kernel, out_shape=(jax.ShapeDtypeStruct((4, 2048), F32), j...]
where the time goes in v7:
time: 131 us; the launch traced here: 129 us
  Pallas kernels  126 us (96%)
  local copies, waits for them, and re-layouts  2.75 us (2%)
    pallas_call x1, Pallas kernels, local(): pl.pallas_call(kernel, out_shape=(jax.ShapeDtypeStruct((4, 2048), F32), j...  126 us
    unnamed x2, local copies, waits for them, and re-layouts  2.75 us

profile of v7, /device:TPU:2, one launch (start us, length us, event | category | flops | bytes accessed | tf_op | source)
XLA Modules:
  0.0 129.5 jit_solution(6074094610164782104)
XLA Ops:
  0.6 126.1 %shard_map.122 = (f32[4,2048]{1,0:T(4,128)}, f32[8,1024]{1,0:T(8,128)}) custom-call(bf16[128,1024]{1,0:T(8,128)(2,1)} %bitcast.6, bf16[128,1024]{1,0:T(8,128)(2,1)} %bitcast.7, bf16[96,2048]{1,0:T(8,128)(2,1)} %bitcast.5, s32[1,96]{1,0:T(1,128)} %bitcast.8, s32[1,96]{1,0:T(1,128)} %bitcast.9, bf16[256,1024]{1,0:T(8,128)(2,1)} %wq_hbm.1, ...), custom_call_target="tpu_custom_call" | custom-call | tf_op jit(solution)/shard_map/pallas_call | solution.py:854
  126.7 1.4 %copy.15 = f32[4,2048]{1,0:T(4,128)} copy(f32[4,2048]{1,0:T(4,128)} %get-tuple-element.4) | data formatting | bytes 65536
  128.1 1.4 %copy.16 = f32[8,1024]{1,0:T(8,128)} copy(f32[8,1024]{1,0:T(8,128)} %get-tuple-element.5) | data formatting | bytes 65536

commit v8 on v7

--- a/solution.py
+++ b/solution.py
@@ -176,9 +176,9 @@
     pieces = (
         (wq_hbm, wq, 0, 1024, "x"),
         (wc_hbm, wc, 0, 1024, "x"),
-        (wkv_hbm, wkv, 0, 1536, "xz"),
-        (wkv_hbm, wkv, 1536, 1536, "zx"),
-        (wa_hbm, wa, 0, 1024, "x"),
+        (wkv_hbm, wkv, 0, 1536, "x"),
+        (wkv_hbm, wkv, 1536, 1536, "xz"),
+        (wa_hbm, wa, 0, 1024, "zx"),
     )
     place_of = {"x": (x + core) % 2, "z": (z + core) % 2}
     mate_of = {
@@ -311,6 +311,10 @@
     lax.fori_loop(0, 192, place, 0, unroll=8)
     pl.semaphore_wait(entered, 7)
     start_piece(0)
+    start_piece(1)
+    start_piece(2)
+    start_piece(3)
+    start_piece(4)
 
     def send_obs(k, carry):
         to = (sp + k) % 64
@@ -326,8 +330,6 @@
         return carry
 
     lax.fori_loop(1, 64, send_obs, 0)
-    start_piece(1)
-    start_piece(2)
     obs_recv[pl.ds(sp * 3, 3)] = obs_send[pl.ds(sp * 3, 3)]
     patch_recv[sp] = slot_patch[sp]
 
@@ -365,7 +367,6 @@
     advance(0, 1)
     advance(1, 1)
     advance(0, 2)
-    start_piece(3)
     finish_piece(0)
 
     def columns(count, width, source, weight, target, offset):
@@ -378,9 +379,10 @@
 
     columns(4, 256, normed, wq, queries, 0)
     advance(2, 1)
-    start_piece(4)
     advance(1, 2)
     advance(2, 2)
+    advance(3, 1)
+    advance(4, 1)
 
     await_bytes(obs_recv.at[pl.ds(0, 189)], bulk_recv.at[0])
     await_bytes(patch_recv.at[pl.ds(0, 63)], bulk_recv.at[1])
@@ -418,9 +420,8 @@
     def cross_four(i, carry):
         @pl.when(i == 1)
         def _():
-            advance(2, 3)
-            advance(3, 1)
-            advance(4, 1)
+            advance(3, 2)
+            advance(4, 2)
 
         for g in range(4):
             cross_pair(i * 4 + g, 0)
@@ -438,8 +439,8 @@
         return carry
 
     lax.fori_loop(0, 4, cross_out, 0)
-    advance(3, 2)
-    advance(4, 2)
+    advance(3, 3)
+    advance(4, 3)
     normed_axial = normalize(after_cross[...]).astype(BF)
     finish_piece(2)
     columns(6, 256, normed_axial, wkv, axial, 0)
@@ -461,7 +462,6 @@
     lax.fori_loop(1, 32, send_lat, 0)
     lat_own[chip] = axial[pl.ds(mult(cell_at * 16, 16), 16), pl.ds(mult(group_at * 384, 128), 384)]
 
-    advance(3, 3)
     finish_piece(3)
     columns(6, 256, normed_axial, wkv, axial, 1536)
 

time: 131 us -> 130 us (level)
  no operation moved by 1% of the time
where the time goes in v8:
time: 130 us; the launch traced here: 129 us
  Pallas kernels  125 us (96%)
  local copies, waits for them, and re-layouts  2.75 us (2%)
    pallas_call x1, Pallas kernels, local(): pl.pallas_call(kernel, out_shape=(jax.ShapeDtypeStruct((4, 2048), F32), j...  125 us
    unnamed x2, local copies, waits for them, and re-layouts  2.75 us

profile of v8, /device:TPU:2, one launch (start us, length us, event | category | flops | bytes accessed | tf_op | source)
XLA Modules:
  0.0 128.7 jit_solution(11486242496813801349)
XLA Ops:
  0.6 125.3 %shard_map.122 = (f32[4,2048]{1,0:T(4,128)}, f32[8,1024]{1,0:T(8,128)}) custom-call(bf16[128,1024]{1,0:T(8,128)(2,1)} %bitcast.6, bf16[128,1024]{1,0:T(8,128)(2,1)} %bitcast.7, bf16[96,2048]{1,0:T(8,128)(2,1)} %bitcast.5, s32[1,96]{1,0:T(1,128)} %bitcast.8, s32[1,96]{1,0:T(1,128)} %bitcast.9, bf16[256,1024]{1,0:T(8,128)(2,1)} %wq_hbm.1, ...), custom_call_target="tpu_custom_call" | custom-call | tf_op jit(solution)/shard_map/pallas_call | solution.py:854
  125.9 1.4 %copy.15 = f32[4,2048]{1,0:T(4,128)} copy(f32[4,2048]{1,0:T(4,128)} %get-tuple-element.4) | data formatting | bytes 65536
  127.3 1.4 %copy.16 = f32[8,1024]{1,0:T(8,128)} copy(f32[8,1024]{1,0:T(8,128)} %get-tuple-element.5) | data formatting | bytes 65536
